TPU v7x, 32 devices: a whole 2x2x4 slice. The times are simulated.
32 devices in a mesh: replica: 16 (over z, y, x), shard: 2 (over core).
Axes of the slice: x: 2, y: 2, z: 4, core: 2. Of those that a mesh axis runs over, the one named last changes fastest.
Arguments:
- layer_input: bfloat16 [16384, 960], P(('replica', 'shard')), may hold values from -6 to 6
- segment_ids: int32 [32, 512], P(('replica', 'shard')), may hold values from 0 to 2, never falling along the last dimension, each value on 1 to 384 neighbouring positions
- upstream_grad: bfloat16 [16384, 960], P(('replica', 'shard')), may hold values from -6 to 6
- attn_gain: bfloat16 [960], P('shard'), may hold values from 0.5 to 1.5
- query_weight: bfloat16 [960, 960], P('shard'), may hold values from -0.1875 to 0.1875
- key_weight: bfloat16 [960, 320], P('shard'), may hold values from -0.1875 to 0.1875
- value_weight: bfloat16 [960, 320], P('shard'), may hold values from -0.1875 to 0.1875
- output_weight: bfloat16 [960, 960], P('shard'), may hold values from -2 to 2
- ffn_gain: bfloat16 [960], P('shard'), may hold values from 0.5 to 1.5
- gate_weight: bfloat16 [960, 2560], P(None, 'shard'), may hold values from -0.1875 to 0.1875
- up_weight: bfloat16 [960, 2560], P(None, 'shard'), may hold values from -0.1875 to 0.1875
- down_weight: bfloat16 [2560, 960], P('shard'), may hold values from -0.125 to 0.125
Outputs:
- layer_output: bfloat16 [16384, 960], P(('replica', 'shard'))
- input_grad: float32 [16384, 960], P(('replica', 'shard'))
- attn_gain_grad: float32 [960], P('shard')
- query_weight_grad: float32 [960, 960], P('shard')
- key_weight_grad: float32 [960, 320], P('shard')
- value_weight_grad: float32 [960, 320], P('shard')
- output_weight_grad: float32 [960, 960], P('shard')
- ffn_gain_grad: float32 [960], P('shard')
- gate_weight_grad: float32 [960, 2560], P(None, 'shard')
- up_weight_grad: float32 [960, 2560], P(None, 'shard')
- down_weight_grad: float32 [2560, 960], P('shard')
Inputs may be any that keep to these rules, and one draw needn't show every extreme that they name: `segment_ids`: in each row the numbers never fall, every one of 0 to 2 appears, and some document in every draw is 384 tokens long.
All inputs are finite; a program needn't handle non-finite values.
Results may differ from a plain program's by a relative error of at most 0.02.
Values may be sent and summed in bfloat16 or wider, within the bound.
A program may use at most 128 MiB of HBM per device.

v0:
```python
import jax
import jax.numpy as jnp
from jax import lax
from jax.sharding import PartitionSpec as P

QUERY_HEADS = 15
KEY_VALUE_HEADS = 5
HEAD_SIZE = 64
SEGS = 3


EPSILON = 1e-05
NEGATIVE = -1e30


def product(left, right):
    return jnp.dot(left, right, preferred_element_type=jnp.float32)


def left_inner(left, right):
    return lax.dot_general(
        left, right, (((0,), (0,)), ((), ())), preferred_element_type=jnp.float32
    )


def right_inner(left, right):
    return lax.dot_general(
        left, right, (((1,), (1,)), ((), ())), preferred_element_type=jnp.float32
    )


def normalize(values):
    inverse = lax.rsqrt(jnp.mean(values * values, -1, keepdims=True) + EPSILON)
    return (values * inverse, inverse)


def norm_backward(grad_norm, normed, inverse):
    return inverse * (grad_norm - normed * jnp.mean(grad_norm * normed, -1, keepdims=True))


def positions_of(segment):
    labels = jnp.arange(SEGS, dtype=jnp.int32)
    onehot = (segment[:, None] == labels[None, :]).astype(jnp.int32)
    counts = jnp.sum(onehot, 0)
    starts = jnp.cumsum(counts) - counts
    first_index = jnp.sum(onehot * starts[None, :], 1)
    return jnp.arange(segment.shape[0], dtype=jnp.int32) - first_index


def rope_tables(segment):
    position = positions_of(segment).astype(jnp.float32)
    half_size = HEAD_SIZE // 2
    frequency = 10000.0 ** (-jnp.arange(half_size, dtype=jnp.float32) * 2.0 / HEAD_SIZE)
    angle = position[:, None] * frequency[None, :]
    cosine = jnp.concatenate([jnp.cos(angle), jnp.cos(angle)], 1)
    sine = jnp.concatenate([-jnp.sin(angle), jnp.sin(angle)], 1)
    return (cosine, sine)


def rotate(values, cosine, sine, sign):
    token_stack = values.shape[0]
    heads = values.shape[1] // HEAD_SIZE
    shaped = values.reshape(token_stack, heads, 2, HEAD_SIZE // 2)
    swapped = shaped[:, :, ::-1, :].reshape(token_stack, heads, HEAD_SIZE)
    plain = values.reshape(token_stack, heads, HEAD_SIZE)
    return (plain * cosine[:, None, :] + sign * swapped * sine[:, None, :]).reshape(
        token_stack, heads * HEAD_SIZE
    )


def allowed_block(start_row, block_rows, segment):
    token_stack = segment.shape[0]
    row_index = start_row + jnp.arange(block_rows, dtype=jnp.int32)
    column_index = jnp.arange(token_stack, dtype=jnp.int32)
    return (column_index[None, :] <= row_index[:, None]) & (segment[None, :] == segment[:, None])


def split_heads(query_reduced, key_reduced, value_reduced):
    token_stack = query_reduced.shape[0]
    shard_groups = QUERY_HEADS // KEY_VALUE_HEADS
    heads_of_query = query_reduced.reshape(
        token_stack, KEY_VALUE_HEADS, shard_groups, HEAD_SIZE
    ).transpose(1, 2, 0, 3)
    heads_of_key = key_reduced.reshape(token_stack, KEY_VALUE_HEADS, HEAD_SIZE).transpose(1, 0, 2)
    heads_of_value = value_reduced.reshape(token_stack, KEY_VALUE_HEADS, HEAD_SIZE).transpose(
        1, 0, 2
    )
    return (heads_of_query, heads_of_key, heads_of_value)


def block_scores(query_rows, key_head, start_row, segment):
    scores = jnp.einsum(
        "gqd,kd->gqk", query_rows, key_head, preferred_element_type=jnp.float32
    ) * HEAD_SIZE ** (-0.5)
    allowed = allowed_block(start_row, query_rows.shape[1], segment)
    return jnp.where(allowed[None], scores, NEGATIVE)


def attention_forward(query_reduced, key_reduced, value_reduced, segment):
    token_stack = query_reduced.shape[0]
    block_rows = min(512, token_stack)
    block_count = token_stack // block_rows
    heads_of_query, heads_of_key, heads_of_value = split_heads(
        query_reduced, key_reduced, value_reduced
    )

    def one_head(operands):
        query_head, key_head, value_head = operands

        def one_block(block_index):
            start_row = block_index * block_rows
            scores = block_scores(query_head, key_head, start_row, segment)
            highest = jnp.max(scores, -1, keepdims=True)
            expo = jnp.exp(scores - highest)
            total = jnp.sum(expo, -1, keepdims=True)
            probs = (expo / total).astype(jnp.bfloat16)
            block_out = jnp.einsum(
                "gqk,kd->gqd", probs, value_head, preferred_element_type=jnp.float32
            )
            return (block_out, (highest + jnp.log(total))[..., 0])

        return lax.map(one_block, jnp.arange(block_count, dtype=jnp.int32))

    head_outs, log_totals = lax.map(one_head, (heads_of_query, heads_of_key, heads_of_value))
    mixed = head_outs.transpose(1, 3, 0, 2, 4).reshape(token_stack, QUERY_HEADS * HEAD_SIZE)
    return (mixed.astype(jnp.bfloat16), log_totals)


def attention_backward(
    query_reduced, key_reduced, value_reduced, gradient_reduced, log_totals, segment
):
    token_stack = query_reduced.shape[0]
    block_rows = min(512, token_stack)
    block_count = token_stack // block_rows
    shard_groups = QUERY_HEADS // KEY_VALUE_HEADS
    scale = HEAD_SIZE ** (-0.5)
    heads_of_query, heads_of_key, heads_of_value = split_heads(
        query_reduced, key_reduced, value_reduced
    )
    head_gradients = gradient_reduced.reshape(
        token_stack, KEY_VALUE_HEADS, shard_groups, HEAD_SIZE
    ).transpose(1, 2, 0, 3)

    def one_head(operands):
        query_head, key_head, value_head, grad_head, total_head = operands

        def one_block(carry, block_index):
            key_acc, value_acc = carry
            start_row = block_index * block_rows
            scores = block_scores(query_head, key_head, start_row, segment)
            probs = jnp.exp(scores - total_head[block_index][..., None])
            grad_probs = jnp.einsum(
                "gqd,kd->gqk", grad_head, value_head, preferred_element_type=jnp.float32
            )
            centre = jnp.sum(probs * grad_probs, -1, keepdims=True)
            grad_scores = (probs * (grad_probs - centre)).astype(jnp.bfloat16)
            query_part = (
                jnp.einsum("gqk,kd->gqd", grad_scores, key_head, preferred_element_type=jnp.float32)
                * scale
            )
            key_acc = (
                key_acc
                + jnp.einsum(
                    "gqk,gqd->kd", grad_scores, query_head, preferred_element_type=jnp.float32
                )
                * scale
            )
            value_acc = value_acc + jnp.einsum(
                "gqk,gqd->kd",
                probs.astype(jnp.bfloat16),
                grad_head,
                preferred_element_type=jnp.float32,
            )
            return ((key_acc, value_acc), query_part)

        zeros = jnp.zeros((token_stack, HEAD_SIZE), jnp.float32)
        (key_gradient, value_gradient), query_blocks = lax.scan(
            one_block, (zeros, zeros), jnp.arange(block_count, dtype=jnp.int32)
        )
        return (query_blocks, key_gradient, value_gradient)

    query_all, gathered_keys, gathered_values = lax.map(
        one_head, (heads_of_query, heads_of_key, heads_of_value, head_gradients, log_totals)
    )
    query_grad = query_all.transpose(1, 3, 0, 2, 4).reshape(token_stack, QUERY_HEADS * HEAD_SIZE)
    key_gradient = gathered_keys.transpose(1, 0, 2).reshape(
        token_stack, KEY_VALUE_HEADS * HEAD_SIZE
    )
    value_gradient = gathered_values.transpose(1, 0, 2).reshape(
        token_stack, KEY_VALUE_HEADS * HEAD_SIZE
    )
    return (query_grad, key_gradient, value_gradient)


def per_device(
    layer_input,
    segment_ids,
    upstream_grad,
    attn_gain,
    query_weight,
    key_weight,
    value_weight,
    output_weight,
    ffn_gain,
    gate_weight,
    up_weight,
    down_weight,
):
    segment = segment_ids.reshape(-1)
    gain_one, gain_two, query_w, key_w, value_w, output_w = (
        lax.all_gather(attn_gain, "shard", axis=0, tiled=True),
        lax.all_gather(ffn_gain, "shard", axis=0, tiled=True),
        lax.all_gather(query_weight, "shard", axis=0, tiled=True),
        lax.all_gather(key_weight, "shard", axis=0, tiled=True),
        lax.all_gather(value_weight, "shard", axis=0, tiled=True),
        lax.all_gather(output_weight, "shard", axis=0, tiled=True),
    )
    gain_one = gain_one.astype(jnp.float32)
    gain_two = gain_two.astype(jnp.float32)
    start_input = layer_input.astype(jnp.float32)
    normed_one, inverse_one = normalize(start_input)
    hidden_one = (normed_one * gain_one).astype(jnp.bfloat16)
    query_val = product(hidden_one, query_w)
    key_tensor = product(hidden_one, key_w)
    value_reduced = product(hidden_one, value_w).astype(jnp.bfloat16)
    cosine, sine = rope_tables(segment)
    query_reduced = rotate(query_val, cosine, sine, 1.0).astype(jnp.bfloat16)
    key_reduced = rotate(key_tensor, cosine, sine, 1.0).astype(jnp.bfloat16)
    mixed_low, log_totals = attention_forward(query_reduced, key_reduced, value_reduced, segment)
    middle = start_input + product(mixed_low, output_w)
    normed_two, inverse_two = normalize(middle)
    hidden_two = (normed_two * gain_two).astype(jnp.bfloat16)
    grad_out = upstream_grad.astype(jnp.float32)
    gate_w, up_w, down_w = (
        lax.all_gather(gate_weight, "shard", axis=1, tiled=True),
        lax.all_gather(up_weight, "shard", axis=1, tiled=True),
        lax.all_gather(down_weight, "shard", axis=0, tiled=True),
    )
    gate_value = product(hidden_two, gate_w)
    up_value = product(hidden_two, up_w)
    sigma = jax.nn.sigmoid(gate_value)
    activ_low = (gate_value * sigma * up_value).astype(jnp.bfloat16)
    layer_output = (middle + product(activ_low, down_w)).astype(jnp.bfloat16)
    gate_again, up_again, down_again = (
        lax.all_gather(gate_weight, "shard", axis=1, tiled=True),
        lax.all_gather(up_weight, "shard", axis=1, tiled=True),
        lax.all_gather(down_weight, "shard", axis=0, tiled=True),
    )
    down_part = left_inner(activ_low, upstream_grad)
    grad_activ = right_inner(upstream_grad, down_again)
    grad_gate = (grad_activ * up_value * sigma * (1.0 + gate_value * (1.0 - sigma))).astype(
        jnp.bfloat16
    )
    grad_up = (grad_activ * gate_value * sigma).astype(jnp.bfloat16)
    gate_part = left_inner(hidden_two, grad_gate)
    up_part = left_inner(hidden_two, grad_up)
    grad_hidden_two = right_inner(grad_gate, gate_again) + right_inner(grad_up, up_again)
    gate_grad, up_grad, down_grad = (
        lax.psum_scatter(
            gate_part.astype(jnp.bfloat16), "shard", scatter_dimension=1, tiled=True
        ).astype(jnp.float32),
        lax.psum_scatter(
            up_part.astype(jnp.bfloat16), "shard", scatter_dimension=1, tiled=True
        ).astype(jnp.float32),
        lax.psum_scatter(
            down_part.astype(jnp.bfloat16), "shard", scatter_dimension=0, tiled=True
        ).astype(jnp.float32),
    )
    gain_two_part = jnp.sum(grad_hidden_two * normed_two, 0)
    grad_middle = grad_out + norm_backward(grad_hidden_two * gain_two, normed_two, inverse_two)
    grad_middle_low = grad_middle.astype(jnp.bfloat16)
    query_again, key_again, value_again, output_again = (
        lax.all_gather(query_weight, "shard", axis=0, tiled=True),
        lax.all_gather(key_weight, "shard", axis=0, tiled=True),
        lax.all_gather(value_weight, "shard", axis=0, tiled=True),
        lax.all_gather(output_weight, "shard", axis=0, tiled=True),
    )
    output_part = left_inner(mixed_low, grad_middle_low)
    grad_mixed = right_inner(grad_middle_low, output_again).astype(jnp.bfloat16)
    grad_query_rot, grad_key_rot, grad_value = attention_backward(
        query_reduced, key_reduced, value_reduced, grad_mixed, log_totals, segment
    )
    grad_query = rotate(grad_query_rot, cosine, sine, -1.0).astype(jnp.bfloat16)
    grad_key = rotate(grad_key_rot, cosine, sine, -1.0).astype(jnp.bfloat16)
    grad_value_low = grad_value.astype(jnp.bfloat16)
    query_part = left_inner(hidden_one, grad_query)
    key_part = left_inner(hidden_one, grad_key)
    value_part = left_inner(hidden_one, grad_value_low)
    grad_hidden_one = (
        right_inner(grad_query, query_again)
        + right_inner(grad_key, key_again)
        + right_inner(grad_value_low, value_again)
    )
    gain_one_part = jnp.sum(grad_hidden_one * normed_one, 0)
    input_grad = grad_middle + norm_backward(grad_hidden_one * gain_one, normed_one, inverse_one)
    gain_one_grad, gain_two_grad, query_grad, key_gradient, value_gradient, output_grad = (
        lax.psum_scatter(
            gain_one_part.astype(jnp.bfloat16), "shard", scatter_dimension=0, tiled=True
        ).astype(jnp.float32),
        lax.psum_scatter(
            gain_two_part.astype(jnp.bfloat16), "shard", scatter_dimension=0, tiled=True
        ).astype(jnp.float32),
        lax.psum_scatter(
            query_part.astype(jnp.bfloat16), "shard", scatter_dimension=0, tiled=True
        ).astype(jnp.float32),
        lax.psum_scatter(
            key_part.astype(jnp.bfloat16), "shard", scatter_dimension=0, tiled=True
        ).astype(jnp.float32),
        lax.psum_scatter(
            value_part.astype(jnp.bfloat16), "shard", scatter_dimension=0, tiled=True
        ).astype(jnp.float32),
        lax.psum_scatter(
            output_part.astype(jnp.bfloat16), "shard", scatter_dimension=0, tiled=True
        ).astype(jnp.float32),
    )
    summed = (
        lax.psum(gain_one_grad.astype(jnp.bfloat16), "replica").astype(jnp.float32),
        lax.psum(query_grad.astype(jnp.bfloat16), "replica").astype(jnp.float32),
        lax.psum(key_gradient.astype(jnp.bfloat16), "replica").astype(jnp.float32),
        lax.psum(value_gradient.astype(jnp.bfloat16), "replica").astype(jnp.float32),
        lax.psum(output_grad.astype(jnp.bfloat16), "replica").astype(jnp.float32),
        lax.psum(gain_two_grad.astype(jnp.bfloat16), "replica").astype(jnp.float32),
        lax.psum(gate_grad.astype(jnp.bfloat16), "replica").astype(jnp.float32),
        lax.psum(up_grad.astype(jnp.bfloat16), "replica").astype(jnp.float32),
        lax.psum(down_grad.astype(jnp.bfloat16), "replica").astype(jnp.float32),
    )
    return (
        layer_output,
        input_grad,
        summed[0],
        summed[1],
        summed[2],
        summed[3],
        summed[4],
        summed[5],
        summed[6],
        summed[7],
        summed[8],
    )


def solution(mesh):
    placed = (
        P(("replica", "shard"), None),
        P(("replica", "shard"), None),
        P(("replica", "shard"), None),
        P("shard"),
        P("shard", None),
        P("shard", None),
        P("shard", None),
        P("shard", None),
        P("shard"),
        P(None, "shard"),
        P(None, "shard"),
        P("shard", None),
    )
    return jax.shard_map(
        per_device,
        mesh=mesh,
        in_specs=placed,
        out_specs=(
            P(("replica", "shard"), None),
            P(("replica", "shard"), None),
            P("shard"),
            P("shard", None),
            P("shard", None),
            P("shard", None),
            P("shard", None),
            P("shard"),
            P(None, "shard"),
            P(None, "shard"),
            P("shard", None),
        ),
        check_vma=False,
    )
```

profile of v0, /device:TPU:0, one launch (start us, length us, event | category | flops | bytes accessed | tf_op | source)
XLA Modules:
  0.0 588.8 jit_solution(12771090048988003999)
XLA Ops:
  28.3 4.2 fusion.79
  38.4 24.3 %while.32 = (s32[]{:T(128)}, bf16[5,1,3,512,64]{3,4,2,1,0:T(8,128)(2,1)}, f32[5,1,3,512]{3,2,1,0:T(4,128)}, s32[1,512]{1,0:T(1,128)S(1)}, bf16[5,3,512,64]{2,3,1...) while((s32[]{:T(128)}, ...), condition=%wide.region_7.8_spmd.clone, body=%wide.region_4.7_spmd.sunk.clone | while | flops 211548672 | bytes 11262541 | solution.py:124
  62.6 3.5 multiply_reduce_fusion.3
  67.8 7.1 %fusion.82 = f32[512,2560]{1,0:T(8,128)} fusion(bf16[512,960]{0,1:T(8,128)(2,1)S(1)} %multiply_convert_fusion.4, bf16[960,2560]{1,0:T(8,128)(2,1)} %all-gather.12.cloned.1.call-done), kind=kOutput, calls=%fused_computation.132 | convolution fusion | flops 2516582400 | bytes 11141120 | tf_op jit(solution)/shard_map/dot_general | solution.py:17
  74.9 7.1 %fusion.83 = f32[512,2560]{1,0:T(8,128)} fusion(bf16[512,960]{0,1:T(8,128)(2,1)S(1)} %multiply_convert_fusion.4, bf16[960,2560]{1,0:T(8,128)(2,1)} %all-gather.14.cloned.1.call-done), kind=kOutput, calls=%fused_computation.133 | convolution fusion | flops 2516582400 | bytes 11141120 | tf_op jit(solution)/shard_map/dot_general | solution.py:17
  82.0 6.0 %all-gather.16.cloned.1.call-done = bf16[2560,960]{0,1:T(8,128)(2,1)} async-done(((bf16[1280,960]{0,1:T(8,128)(2,1)}), bf16[2560,960]{0,1:T(8,128)(2,1)}) %all-gather.16.cloned.1.call-update) | async-done | bytes 4915216 | tf_op jit(solution)/shard_map/all_gather | solution.py:237
  88.0 10.5 %multiply_convert_fusion.1 = (bf16[512,2560]{1,0:T(8,128)(2,1)S(1)}, bf16[512,2560]{1,0:T(8,128)(2,1)S(1)}, bf16[512,2560]{1,0:T(8,128)(2,1)}) fusion(f32[512,2560]{1,0:T(8,128)} %fusion.82, f32[512,2560]{1,0:T(8,128)} %fusion.83, bf16[512,960]{0,1:T(8,128)(2,1)} %param.18, bf16[2560,960]{0,1:T(8,128)(2,1)} %all-gather.16.cloned.1.call-done), kind=kOutput, calls=%fused_computation.62 | convolution fusion | flops 2537553920 | bytes 24248320 | tf_op jit(solution)/shard_map/dot_general | solution.py:27
  98.5 6.8 %fusion.84 = f32[512,960]{0,1:T(8,128)S(1)} fusion(bf16[512,2560]{1,0:T(8,128)(2,1)S(1)} %get-tuple-element.340, bf16[960,2560]{1,0:T(8,128)(2,1)} %all-gather.12.cloned.1.call-done), kind=kOutput, calls=%fused_computation.134 | convolution fusion | flops 2516582400 | bytes 9502720 | tf_op jit(solution)/shard_map/dot_general | solution.py:27
  105.3 3.7 multiply_reduce_fusion.1
  112.7 44.6 %while.44 = (s32[]{:T(128)}, f32[5,1,3,512,64]{3,4,2,1,0:T(8,128)}, f32[5,512,64]{1,2,0:T(8,128)}, bf16[5,512,64]{1,2,0:T(8,128)(2,1)}, s32[1,512]{1,0:T(1,128)S...) while((s32[]{:T(128)}, f32[5,1,3,512,64]{3,4,2,1,0:T(8,128)}, ...), condition=%wide.region_12.13_spmd.clone, body=%wide.region_10.12_spmd.sunk.clone | while | flops 511310336 | bytes 25795688 | solution.py:182
  164.5 4.4 convolution_convert_fusion.3
  178.2 6.4 %convolution_convert_fusion.2 = bf16[960,2560]{1,0:T(8,128)(2,1)} fusion(bf16[512,960]{0,1:T(8,128)(2,1)S(1)} %multiply_convert_fusion.4, bf16[512,2560]{1,0:T(8,128)(2,1)} %copy-done.37), kind=kOutput, calls=%fused_computation.61 | convolution fusion | flops 2519040000 | bytes 8519680 | tf_op jit(solution)/shard_map/dot_general | solution.py:21
  184.7 6.1 %convolution_convert_fusion.1 = bf16[960,2560]{1,0:T(8,128)(2,1)} fusion(bf16[512,960]{0,1:T(8,128)(2,1)S(1)} %multiply_convert_fusion.4, bf16[512,2560]{1,0:T(8,128)(2,1)} %copy-done.36), kind=kOutput, calls=%fused_computation.60 | convolution fusion | flops 2519040000 | bytes 8519680 | tf_op jit(solution)/shard_map/dot_general | solution.py:21
  192.0 6.1 %convolution_convert_fusion = bf16[2560,960]{0,1:T(8,128)(2,1)} fusion(bf16[512,960]{0,1:T(8,128)(2,1)S(1)} %copy-done.18, bf16[512,2560]{1,0:T(8,128)(2,1)} %get-tuple-element.341), kind=kOutput, calls=%fused_computation.59 | convolution fusion | flops 2519040000 | bytes 8519680 | tf_op jit(solution)/shard_map/dot_general | solution.py:21
  202.0 7.2 %reduce-scatter.12.cloned.1.call-done = bf16[480,960]{1,0:T(8,128)(2,1)} async-done(((bf16[960,960]{1,0:T(8,128)(2,1)}), bf16[480,960]{1,0:T(8,128)(2,1)}) %reduce-scatter.12.cloned.1.call-update) | async-done | bytes 921616 | tf_op jit(solution)/shard_map/reduce_scatter | solution.py:303
  209.2 16.8 %reduce-scatter.16.cloned.1.call-done = bf16[960,1280]{1,0:T(8,128)(2,1)} async-done(((bf16[960,2560]{1,0:T(8,128)(2,1)}), bf16[960,1280]{1,0:T(8,128)(2,1)}) %reduce-scatter.16.cloned.1.call-update) | async-done | bytes 2457616 | tf_op jit(solution)/shard_map/reduce_scatter | solution.py:259
  225.9 17.0 %reduce-scatter.18.cloned.1.call-done = bf16[960,1280]{1,0:T(8,128)(2,1)} async-done(((bf16[960,2560]{1,0:T(8,128)(2,1)}), bf16[960,1280]{1,0:T(8,128)(2,1)}) %reduce-scatter.18.cloned.1.call-update) | async-done | bytes 2457616 | tf_op jit(solution)/shard_map/reduce_scatter | solution.py:262
  243.0 16.8 %reduce-scatter.20.cloned.1.call-done = bf16[1280,960]{0,1:T(8,128)(2,1)} async-done(((bf16[2560,960]{0,1:T(8,128)(2,1)}), bf16[1280,960]{0,1:T(8,128)(2,1)}) %reduce-scatter.20.cloned.1.call-update) | async-done | bytes 2457616 | tf_op jit(solution)/shard_map/reduce_scatter | solution.py:265
  264.9 3.4 fusion.60
  270.9 44.1 %all-reduce.4 = (bf16[480]{0:T(512)(128)(2,1)S(1)}, bf16[480]{0:T(512)(128)(2,1)S(1)}) all-reduce(bf16[480]{0:T(512)(128)(2,1)S(1)} %dynamic-slice.3, bf16[480]{0:T(512)(128)(2,1)S(1)} %dynamic-slice.5), channel_id=1, replica_groups=mesh['replica'=16,'shard'=2] {'replica'}, use_global_device_ids=true, to_apply=%region_16.17 | all-reduce | flops 960 | bytes 3840 | tf_op jit(solution)/shard_map/psum | solution.py:317
  316.2 4.4 fusion.59
  320.6 6.2 %add_convert_fusion = bf16[512,960]{0,1:T(8,128)(2,1)} fusion(f32[512,960]{0,1:T(8,128)S(1)} %copy-done.3, bf16[512,2560]{1,0:T(8,128)(2,1)S(1)} %copy-done.35, bf16[2560,960]{0,1:T(8,128)(2,1)} %all-gather.16.cloned.1.call-done), kind=kOutput, calls=%fused_computation.92 | convolution fusion | flops 2517565440 | bytes 10485760 | tf_op jit(solution)/shard_map/dot_general | solution.py:17
  326.7 240.6 %all-reduce.10.cloned.1.call-done = (bf16[480,960]{1,0:T(8,128)(2,1)}, bf16[480,320]{0,1:T(8,128)(2,1)}, bf16[480,320]{0,1:T(8,128)(2,1)}, bf16[480,960]{1,0:T(8...) async-done(((bf16[480,960]{1,0:T(8,128)(2,1)}, bf16[480,320]{0,1:T(8,128)(2,1)}, bf16[480,320]{0,1:T(8,128)(2,1)}, ...) | async-done | bytes 9830416 | tf_op jit(solution)/shard_map/psum | solution.py:318
  567.3 4.5 convert_element_type.214
  (240 shorter events, 139.6 us)
Async XLA Ops:
  7.2 21.1 %all-gather.8.cloned.1.call-start = ((), (), s32[]{:S(2)}) async-start(), calls=%async_computation.7 | async-start | bytes 2949120 | tf_op jit(solution)/shard_map/all_gather | solution.py:213
  7.9 54.7 %all-gather.10.cloned.1.call-start = ((), (), s32[]{:S(2)}) async-start(), calls=%async_computation.8 | async-start | bytes 2949120 | tf_op jit(solution)/shard_map/all_gather | solution.py:216
  8.7 59.1 %all-gather.12.cloned.1.call-start = ((), (), s32[]{:S(2)}) async-start(), calls=%async_computation.9 | async-start | bytes 7372800 | tf_op jit(solution)/shard_map/all_gather | solution.py:235
  9.4 65.5 %all-gather.14.cloned.1.call-start = ((), (), s32[]{:S(2)}) async-start(), calls=%async_computation.10 | async-start | bytes 7372800 | tf_op jit(solution)/shard_map/all_gather | solution.py:236
  10.0 6.0 %copy-start = (bf16[512,960]{0,1:T(8,128)(2,1)S(1)}, bf16[512,960]{0,1:T(8,128)(2,1)}, u32[]{:S(2)}) copy-start(bf16[512,960]{0,1:T(8,128)(2,1)} %param.16) | copy-start | bytes 2949124
  10.0 6.3 %copy-start.21 = (bf16[480,320]{0,1:T(8,128)(2,1)S(1)}, bf16[480,320]{0,1:T(8,128)(2,1)}, u32[]{:S(2)}) copy-start(bf16[480,320]{0,1:T(8,128)(2,1)} %param.21) | copy-start | bytes 921604
  10.0 77.9 %all-gather.16.cloned.1.call-start = ((), (), s32[]{:S(2)}) async-start(), calls=%async_computation.11 | async-start | bytes 7372800 | tf_op jit(solution)/shard_map/all_gather | solution.py:237
  10.6 187.6 %reduce-scatter.22.cloned.1.call-start = ((), (), s32[]{:S(2)}) async-start(), calls=%async_computation.17 | async-start | bytes 1105920
  20.5 4.6 copy-start.10
  98.4 6.8 %copy-start.37 = (bf16[512,2560]{1,0:T(8,128)(2,1)}, bf16[512,2560]{1,0:T(8,128)(2,1)S(1)}, u32[]{:S(2)}) copy-start(bf16[512,2560]{1,0:T(8,128)(2,1)S(1)} %get-tuple-element.340) | copy-start | bytes 7864324
  98.4 6.8 %copy-start.36 = (bf16[512,2560]{1,0:T(8,128)(2,1)}, bf16[512,2560]{1,0:T(8,128)(2,1)S(1)}, u32[]{:S(2)}) copy-start(bf16[512,2560]{1,0:T(8,128)(2,1)S(1)} %get-tuple-element.339) | copy-start | bytes 7864324
  98.4 6.8 %copy-start.2 = (f32[512,960]{0,1:T(8,128)S(1)}, f32[512,960]{0,1:T(8,128)}, u32[]{:S(2)}) copy-start(f32[512,960]{0,1:T(8,128)} %copy-done.1) | copy-start | bytes 5898244
  98.4 6.8 %copy-start.5 = (bf16[960,2560]{1,0:T(8,128)(2,1)S(1)}, bf16[960,2560]{1,0:T(8,128)(2,1)}, u32[]{:S(2)}) copy-start(bf16[960,2560]{1,0:T(8,128)(2,1)} %all-gather.14.cloned.1.call-done) | copy-start | bytes 14745604
  98.4 6.8 %copy-start.28 = (f32[512]{0:T(512)S(1)}, f32[512]{0:T(512)}, u32[]{:S(2)}) copy-start(f32[512]{0:T(512)} %copy-done.27) | copy-start | bytes 6148
  161.5 38.6 %reduce-scatter.24.cloned.1.call-start = ((), (), s32[]{:S(2)}) async-start(), calls=%async_computation.18 | async-start | bytes 1105920
  164.4 37.6 %reduce-scatter.14.cloned.1.call-start = ((), (), s32[]{:S(2)}) async-start(), calls=%async_computation.13 | async-start | bytes 2949120 | tf_op jit(solution)/shard_map/reduce_scatter | solution.py:312
  168.9 40.3 %reduce-scatter.12.cloned.1.call-start = ((), (), s32[]{:S(2)}) async-start(), calls=%async_computation.12 | async-start | bytes 2949120 | tf_op jit(solution)/shard_map/reduce_scatter | solution.py:303
  178.2 47.8 %reduce-scatter.16.cloned.1.call-start = ((), (), s32[]{:S(2)}) async-start(), calls=%async_computation.14 | async-start | bytes 7372800 | tf_op jit(solution)/shard_map/reduce_scatter | solution.py:259
  184.6 58.4 %reduce-scatter.18.cloned.1.call-start = ((), (), s32[]{:S(2)}) async-start(), calls=%async_computation.15 | async-start | bytes 7372800 | tf_op jit(solution)/shard_map/reduce_scatter | solution.py:262
  190.8 69.0 %reduce-scatter.20.cloned.1.call-start = ((), (), s32[]{:S(2)}) async-start(), calls=%async_computation.16 | async-start | bytes 7372800 | tf_op jit(solution)/shard_map/reduce_scatter | solution.py:265
  198.2 369.2 %all-reduce.10.cloned.1.call-start = ((), (), s32[]{:S(2)}) async-start(), calls=%async_computation.19 | async-start | bytes 19988480 | tf_op jit(solution)/shard_map/psum | solution.py:318
  316.2 4.4 copy-start.3
  316.2 4.4 copy-start.35
  567.3 4.5 copy-start.14
  (27 other events, 54.0 us)
Sparse Core Ops, SparseCore 0:
  9.6 13.0 all-gather.7
  24.2 11.5 all-gather.9
  37.4 15.8 all-gather.11
  54.7 15.8 all-gather.13
  72.0 15.8 all-gather.15
  161.6 9.3 reduce-scatter.21
  173.3 9.3 reduce-scatter.23
  184.9 10.6 reduce-scatter.13
  198.5 10.6 reduce-scatter.11
  211.9 13.9 reduce-scatter.15
  228.8 14.0 reduce-scatter.17
  245.7 14.0 reduce-scatter.19
  266.8 300.4 all-reduce.9
where the time goes:
time: 596 us; the launch traced here: 589 us
  waiting for transfers between devices  308 us (52%)
  matrix products  139 us (23%)
  blocking collectives  53.7 us (9%)
  other arithmetic  43.3 us (7%)
  local copies, waits for them, and re-layouts  27.8 us (5%)
  between operations  16.1 us (3%)
    psum x1, waiting for transfers between devices, per_device(): lax.psum(query_grad.astype(jnp.bfloat16), 'replica').astype(jnp.float32)  241 us
    psum x1, blocking collectives, per_device(): lax.psum(gain_one_grad.astype(jnp.bfloat16), 'replica').astype(jnp.float32)  44.1 us
    dot_general x7, matrix products, product(): return jnp.dot(left, right, preferred_element_type=jnp.float32)  30 us
    dot_general x7, matrix products, right_inner(): lax.dot_general(left, right, (((1,), (1,)), ((), ())), preferred_element_...  29.6 us
    dot_general x7, matrix products, left_inner(): lax.dot_general(left, right, (((0,), (0,)), ((), ())), preferred_element_...  27.7 us
    reduce_scatter x1, waiting for transfers between devices, per_device(): lax.psum_scatter(up_part.astype(jnp.bfloat16), 'shard', scatter_dimension...  17 us
    reduce_scatter x1, waiting for transfers between devices, per_device(): lax.psum_scatter(down_part.astype(jnp.bfloat16), 'shard', scatter_dimensi...  16.8 us
    reduce_scatter x1, waiting for transfers between devices, per_device(): lax.psum_scatter(gate_part.astype(jnp.bfloat16), 'shard', scatter_dimensi...  16.8 us
  transfers between devices with their start and end apart: 13, of which 6 were waited for; matrix products, arithmetic and copies ran while one was open for 20% of the time, Pallas kernels for 0%

commit v1 on v0

v1 whole, which is shorter than its diff:
```python
import functools

import jax
import jax.numpy as jnp
from jax import lax
from jax.experimental import pallas as pl
from jax.experimental.pallas import tpu as pltpu
from jax.sharding import PartitionSpec as P

QUERY_HEADS = 15
KEY_VALUE_HEADS = 5
HEAD_SIZE = 64
SEGS = 3


EPSILON = 1e-05
NEGATIVE = -1e30


def product(left, right):
    return jnp.dot(left, right, preferred_element_type=jnp.float32)


def left_inner(left, right):
    return lax.dot_general(
        left, right, (((0,), (0,)), ((), ())), preferred_element_type=jnp.float32
    )


def right_inner(left, right):
    return lax.dot_general(
        left, right, (((1,), (1,)), ((), ())), preferred_element_type=jnp.float32
    )


def normalize(values):
    inverse = lax.rsqrt(jnp.mean(values * values, -1, keepdims=True) + EPSILON)
    return (values * inverse, inverse)


def norm_backward(grad_norm, normed, inverse):
    return inverse * (grad_norm - normed * jnp.mean(grad_norm * normed, -1, keepdims=True))


def positions_of(segment):
    labels = jnp.arange(SEGS, dtype=jnp.int32)
    onehot = (segment[:, None] == labels[None, :]).astype(jnp.int32)
    counts = jnp.sum(onehot, 0)
    starts = jnp.cumsum(counts) - counts
    first_index = jnp.sum(onehot * starts[None, :], 1)
    return jnp.arange(segment.shape[0], dtype=jnp.int32) - first_index


GROUP = QUERY_HEADS // KEY_VALUE_HEADS
SCALE = HEAD_SIZE ** (-0.5)


def contract(left, right, left_dim, right_dim):
    return lax.dot_general(
        left,
        right,
        (((left_dim,), (right_dim,)), ((), ())),
        preferred_element_type=jnp.float32,
    )


def rope_tables(segment):
    position = positions_of(segment).astype(jnp.float32)
    half_size = HEAD_SIZE // 2
    frequency = 10000.0 ** (-jnp.arange(half_size, dtype=jnp.float32) * 2.0 / HEAD_SIZE)
    angle = frequency[:, None] * position[None, :]
    return (jnp.cos(angle), jnp.sin(angle))


def rotate(values, cosine, sine):
    features, tokens = values.shape
    shaped = values.reshape(features // HEAD_SIZE, 2, HEAD_SIZE // 2, tokens)
    first, second = shaped[:, 0], shaped[:, 1]
    turned = jnp.stack(
        [first * cosine - second * sine, second * cosine + first * sine], 1
    )
    return turned.reshape(features, tokens)


def row_blocks(tokens):
    if tokens % 256 == 0:
        return [(start, 256, start + 256) for start in range(0, tokens, 256)]
    return [(0, tokens, tokens)]


def masked_probs(key_rows, query_columns, seg_col, seg_row, start):
    scores = contract(key_rows, query_columns, 1, 0) * SCALE
    key_index = lax.broadcasted_iota(jnp.int32, scores.shape, 0)
    query_index = lax.broadcasted_iota(jnp.int32, scores.shape, 1) + start
    allowed = (key_index <= query_index) & (seg_col == seg_row)
    scores = jnp.where(allowed, scores, NEGATIVE)
    expo = jnp.exp(scores - jnp.max(scores, 0, keepdims=True))
    return expo * (1.0 / jnp.sum(expo, 0, keepdims=True))


def forward_kernel(seg_col, seg_row, query, key_rows, value, out):
    tokens = query.shape[1]
    for start, count, keys in row_blocks(tokens):
        for member in range(GROUP):
            rows = slice(member * HEAD_SIZE, (member + 1) * HEAD_SIZE)
            columns = slice(start, start + count)
            probs = masked_probs(
                key_rows[0, :keys, :],
                query[rows, columns],
                seg_col[:keys, :],
                seg_row[:, columns],
                start,
            ).astype(jnp.bfloat16)
            out[rows, columns] = contract(value[:, :keys], probs, 1, 0).astype(jnp.bfloat16)


def backward_kernel(
    seg_col, seg_row, query, key, key_rows, value_rows, grad, query_out, key_out, value_out
):
    tokens = query.shape[1]
    key_out[...] = jnp.zeros_like(key_out)
    value_out[...] = jnp.zeros_like(value_out)
    for start, count, keys in row_blocks(tokens):
        for member in range(GROUP):
            rows = slice(member * HEAD_SIZE, (member + 1) * HEAD_SIZE)
            columns = slice(start, start + count)
            query_head = query[rows, columns]
            grad_head = grad[rows, columns]
            probs = masked_probs(
                key_rows[0, :keys, :], query_head, seg_col[:keys, :], seg_row[:, columns], start
            )
            grad_probs = contract(value_rows[0, :keys, :], grad_head, 1, 0)
            centre = jnp.sum(probs * grad_probs, 0, keepdims=True)
            grad_scores = (probs * (grad_probs - centre)).astype(jnp.bfloat16)
            query_out[rows, columns] = contract(key[:, :keys], grad_scores, 1, 0) * SCALE
            key_out[:, :keys] += contract(query_head, grad_scores, 1, 1) * SCALE
            value_out[:, :keys] += contract(grad_head, probs.astype(jnp.bfloat16), 1, 1)


def head_specs(tokens):
    group = pl.BlockSpec((GROUP * HEAD_SIZE, tokens), lambda j: (j, 0))
    single = pl.BlockSpec((HEAD_SIZE, tokens), lambda j: (j, 0))
    rows = pl.BlockSpec((1, tokens, HEAD_SIZE), lambda j: (j, 0, 0))
    seg_col = pl.BlockSpec((tokens, 1), lambda j: (0, 0))
    seg_row = pl.BlockSpec((1, tokens), lambda j: (0, 0))
    return group, single, rows, seg_col, seg_row


def attention_forward(segment, query, key_rows, value):
    tokens = query.shape[1]
    group, single, rows, seg_col, seg_row = head_specs(tokens)
    work = QUERY_HEADS * tokens * tokens
    return pl.pallas_call(
        forward_kernel,
        grid=(KEY_VALUE_HEADS,),
        out_shape=jax.ShapeDtypeStruct(query.shape, jnp.bfloat16),
        in_specs=[seg_col, seg_row, group, rows, single],
        out_specs=group,
        compiler_params=pltpu.CompilerParams(vmem_limit_bytes=40 * 2**20),
        cost_estimate=pl.CostEstimate(
            flops=work * HEAD_SIZE * 16, bytes_accessed=3 * 2**20, transcendentals=work
        ),
    )(segment[:, None], segment[None, :], query, key_rows, value)


def attention_backward(segment, query, key, key_rows, value_rows, grad):
    tokens = query.shape[1]
    group, single, rows, seg_col, seg_row = head_specs(tokens)
    work = QUERY_HEADS * tokens * tokens
    return pl.pallas_call(
        backward_kernel,
        grid=(KEY_VALUE_HEADS,),
        out_shape=(
            jax.ShapeDtypeStruct(query.shape, jnp.float32),
            jax.ShapeDtypeStruct(key.shape, jnp.float32),
            jax.ShapeDtypeStruct(key.shape, jnp.float32),
        ),
        in_specs=[seg_col, seg_row, group, single, rows, rows, group],
        out_specs=(group, single, single),
        compiler_params=pltpu.CompilerParams(vmem_limit_bytes=40 * 2**20),
        cost_estimate=pl.CostEstimate(
            flops=work * HEAD_SIZE * 40, bytes_accessed=8 * 2**20, transcendentals=work
        ),
    )(segment[:, None], segment[None, :], query, key, key_rows, value_rows, grad)


def by_rows(values):
    return values.reshape(-1, HEAD_SIZE, values.shape[1]).transpose(0, 2, 1)


def halving_dim(shape):
    if shape[0] % 16 == 0:
        return 0
    if shape[1] % 256 == 0:
        return 1
    return 0 if shape[0] % 2 == 0 else 1


def piece(values, which, dim, size):
    return lax.dynamic_slice_in_dim(values, which * size, size, dim)


def replica_sum(values, order, replicas):
    levels = replicas.bit_length() - 1
    if replicas != 1 << levels:
        return lax.psum(values, "replica").astype(jnp.float32)
    bits = [bit for bit in order if bit < levels]
    bits += [bit for bit in range(levels) if bit not in bits]
    index = lax.axis_index("replica")
    taken = []
    for bit in bits:
        pairs = [(i, i ^ (1 << bit)) for i in range(replicas)]
        dim = halving_dim(values.shape)
        size = values.shape[dim] // 2
        side = (index >> bit) & 1
        arrived = lax.ppermute(piece(values, 1 - side, dim, size), "replica", pairs)
        values = piece(values, side, dim, size) + arrived
        taken.append((pairs, dim, side))
    for pairs, dim, side in reversed(taken):
        arrived = lax.ppermute(values, "replica", pairs)
        low_side = side == 0
        values = jnp.concatenate(
            [jnp.where(low_side, values, arrived), jnp.where(low_side, arrived, values)], dim
        )
    return values.astype(jnp.float32)


def shard_sum(make, dim, full, shards):
    if shards == 2:
        size = full // 2
        side = lax.axis_index("shard")
        sent = make(1 - side, size).astype(jnp.bfloat16)
        arrived = lax.ppermute(sent, "shard", [(0, 1), (1, 0)])
        return (make(side, size) + arrived.astype(jnp.float32)).astype(jnp.bfloat16)
    whole = make(0, full).astype(jnp.bfloat16)
    return lax.psum_scatter(whole, "shard", scatter_dimension=dim, tiled=True)


def per_device(
    replicas,
    shards,
    layer_input,
    segment_ids,
    upstream_grad,
    attn_gain,
    query_weight,
    key_weight,
    value_weight,
    output_weight,
    ffn_gain,
    gate_weight,
    up_weight,
    down_weight,
):
    segment = segment_ids.reshape(-1)
    features = layer_input.shape[1]
    hidden = gate_weight.shape[1] * shards
    query_size, key_size = query_weight.shape[1], key_weight.shape[1]
    gains = lax.all_gather(jnp.stack([attn_gain, ffn_gain]), "shard", axis=1, tiled=True)
    projections = lax.all_gather(
        jnp.concatenate([query_weight, key_weight, value_weight], 1), "shard", axis=0, tiled=True
    )
    output_w = lax.all_gather(output_weight, "shard", axis=0, tiled=True)
    gate_w = lax.all_gather(gate_weight, "shard", axis=1, tiled=True)
    up_w = lax.all_gather(up_weight, "shard", axis=1, tiled=True)
    down_w = lax.all_gather(down_weight, "shard", axis=0, tiled=True)

    gain_one = gains[0].astype(jnp.float32)
    gain_two = gains[1].astype(jnp.float32)
    start_input = layer_input.astype(jnp.float32)
    normed_one, inverse_one = normalize(start_input)
    hidden_one = (normed_one * gain_one).astype(jnp.bfloat16)
    projected = contract(projections, hidden_one, 0, 1)
    cosine, sine = rope_tables(segment)
    turned = rotate(projected[: query_size + key_size], cosine, sine).astype(jnp.bfloat16)
    query, key = turned[:query_size], turned[query_size:]
    value = projected[query_size + key_size :].astype(jnp.bfloat16)
    key_rows, value_rows = by_rows(key), by_rows(value)
    mixed = attention_forward(segment, query, key_rows, value)
    middle = start_input + contract(mixed, output_w, 0, 0)
    normed_two, inverse_two = normalize(middle)
    hidden_two = (normed_two * gain_two).astype(jnp.bfloat16)

    gate_value = product(hidden_two, gate_w)
    up_value = product(hidden_two, up_w)
    sigma = jax.nn.sigmoid(gate_value)
    grad_activ = right_inner(upstream_grad, down_w)
    activ_low = (gate_value * sigma * up_value).astype(jnp.bfloat16)
    grad_gate = (grad_activ * up_value * sigma * (1.0 + gate_value * (1.0 - sigma))).astype(
        jnp.bfloat16
    )
    grad_up = (grad_activ * gate_value * sigma).astype(jnp.bfloat16)

    gate_grad = shard_sum(
        lambda which, size: left_inner(hidden_two, piece(grad_gate, which, 1, size)),
        1,
        hidden,
        shards,
    )
    gate_grad = replica_sum(gate_grad, ORDERS[0], replicas)
    up_grad = shard_sum(
        lambda which, size: left_inner(hidden_two, piece(grad_up, which, 1, size)),
        1,
        hidden,
        shards,
    )
    up_grad = replica_sum(up_grad, ORDERS[1], replicas)
    down_grad = shard_sum(
        lambda which, size: left_inner(piece(activ_low, which, 1, size), upstream_grad),
        0,
        hidden,
        shards,
    )
    down_grad = replica_sum(down_grad, ORDERS[2], replicas)

    layer_output = (middle + product(activ_low, down_w)).astype(jnp.bfloat16)
    grad_hidden_two = right_inner(grad_gate, gate_w) + right_inner(grad_up, up_w)
    gain_two_part = jnp.sum(grad_hidden_two * normed_two, 0)
    grad_middle = upstream_grad.astype(jnp.float32) + norm_backward(
        grad_hidden_two * gain_two, normed_two, inverse_two
    )
    grad_middle_low = grad_middle.astype(jnp.bfloat16)

    rows = features // shards
    padded = -(-(rows + 1) // 128) * 128

    output_part = contract(mixed, grad_middle_low, 1, 0)
    output_grad = shard_sum(
        lambda which, size: piece(output_part, which, 0, size), 0, query_size, shards
    )
    output_grad = jnp.pad(output_grad, ((0, padded - output_grad.shape[0]), (0, 0)))
    output_grad = replica_sum(output_grad, ORDERS[2], replicas)[: query_size // shards]

    grad_mixed = contract(output_w, grad_middle_low, 1, 1).astype(jnp.bfloat16)
    grad_query, grad_key, grad_value = attention_backward(
        segment, query, key, key_rows, value_rows, grad_mixed
    )
    grad_projected = jnp.concatenate(
        [
            rotate(grad_query, cosine, -sine).astype(jnp.bfloat16),
            rotate(grad_key, cosine, -sine).astype(jnp.bfloat16),
            grad_value.astype(jnp.bfloat16),
        ],
        0,
    )
    grad_hidden_one = contract(grad_projected, projections, 0, 1)
    gain_one_part = jnp.sum(grad_hidden_one * normed_one, 0)
    input_grad = grad_middle + norm_backward(grad_hidden_one * gain_one, normed_one, inverse_one)

    projection_part = contract(hidden_one, grad_projected, 0, 1)
    width = projection_part.shape[1]
    gain_parts = jnp.stack([gain_one_part, gain_two_part]).reshape(2, shards, rows)
    gain_rows = gain_parts.transpose(1, 0, 2).reshape(shards, 1, 2 * rows)
    gain_rows = jnp.pad(gain_rows, ((0, 0), (0, padded - rows - 1), (0, width - 2 * rows)))
    packed = jnp.concatenate([projection_part.reshape(shards, rows, width), gain_rows], 1)
    packed = packed.reshape(shards * padded, width)
    packed = shard_sum(
        lambda which, size: piece(packed, which, 0, size), 0, shards * padded, shards
    )
    cuts = [0, width // 384 * 128, width // 384 * 256, width]
    packed = jnp.concatenate(
        [
            replica_sum(packed[:, cuts[i] : cuts[i + 1]], ORDERS[i], replicas)
            for i in range(3)
        ],
        1,
    )
    query_grad = packed[:rows, :query_size]
    key_grad = packed[:rows, query_size : query_size + key_size]
    value_grad = packed[:rows, query_size + key_size :]
    gain_one_grad = packed[rows, :rows]
    gain_two_grad = packed[rows, rows : 2 * rows]
    return (
        layer_output,
        input_grad,
        gain_one_grad,
        query_grad,
        key_grad,
        value_grad,
        output_grad,
        gain_two_grad,
        gate_grad,
        up_grad,
        down_grad,
    )


ORDERS = ((0, 1, 2, 3), (1, 2, 0, 3), (2, 0, 1, 3))


def solution(mesh):
    placed = (
        P(("replica", "shard"), None),
        P(("replica", "shard"), None),
        P(("replica", "shard"), None),
        P("shard"),
        P("shard", None),
        P("shard", None),
        P("shard", None),
        P("shard", None),
        P("shard"),
        P(None, "shard"),
        P(None, "shard"),
        P("shard", None),
    )
    return jax.shard_map(
        functools.partial(per_device, mesh.shape["replica"], mesh.shape["shard"]),
        mesh=mesh,
        in_specs=placed,
        out_specs=(
            P(("replica", "shard"), None),
            P(("replica", "shard"), None),
            P("shard"),
            P("shard", None),
            P("shard", None),
            P("shard", None),
            P("shard", None),
            P("shard"),
            P(None, "shard"),
            P(None, "shard"),
            P("shard", None),
        ),
        check_vma=False,
    )
```

time: 596 us -> 524 us (0.88)
  waiting for transfers between devices: 308 us -> 233 us
  matrix products: 139 us -> 78.3 us
  starting transfers between devices: 0.52 us -> 58.5 us
  blocking collectives: 53.7 us -> 1.93 us
  Pallas kernels: 0 us -> 28.8 us
  local copies, waits for them, and re-layouts: 27.8 us -> 47.1 us
  other arithmetic: 43.3 us -> 55.7 us
    psum x1 -> x0, waiting for transfers between devices: 241 us -> none  [per_device(): lax.psum(query_grad.astype(jnp.bfloat16), 'replica').astype(jnp.float32)]
    ppermute x0 -> x61, waiting for transfers between devices: none -> 198 us  [the longest x28 108 us: replica_sum(): arrived = lax.ppermute(values, 'replica', pairs)]
    ppermute x0 -> x61, starting transfers between devices: none -> 58.3 us  [the longest x28 35 us: replica_sum(): arrived = lax.ppermute(piece(values, 1 - side, dim, size), 'replica', pairs)]
    reduce_scatter x5 -> x0, waiting for transfers between devices: 57.8 us -> none  [the longest x1 17 us: per_device(): lax.psum_scatter(up_part.astype(jnp.bfloat16), 'shard', scatter_dimension...]
    psum x1 -> x0, blocking collectives: 44.1 us -> none  [per_device(): lax.psum(gain_one_grad.astype(jnp.bfloat16), 'replica').astype(jnp.float32)]
    dot_general x35 -> x6, matrix products: 52.1 us -> 19.2 us  [contract(): lax.dot_general(left, right, (((left_dim,), (right_dim,)), ((), ())), pre...]
    pallas_call x0 -> x2, Pallas kernels: none -> 28.8 us  [the longest x1 17.7 us: attention_backward(): pl.pallas_call(backward_kernel, grid=(KEY_VALUE_HEADS,), out_shape=(jax.S...]
    all_gather x5, waiting for transfers between devices: 6.05 us -> 32.9 us  [the longest x1 9.43 us: per_device(): down_w = lax.all_gather(down_weight, 'shard', axis=0, tiled=True)]
  transfers between devices with their start and end apart: 13 -> 66, of which waited for: 6 -> 43; matrix products, arithmetic and copies ran while one was open for 20% -> 24% of each run, Pallas kernels for 0% -> 2%
where the time goes in v1:
time: 524 us; the launch traced here: 519 us
  waiting for transfers between devices  233 us (44%)
  matrix products  78.3 us (15%)
  starting transfers between devices  58.5 us (11%)
  other arithmetic  55.7 us (11%)
  local copies, waits for them, and re-layouts  47.1 us (9%)
  Pallas kernels  28.8 us (5%)
  between operations  15.4 us (3%)
    ppermute x28, waiting for transfers between devices, replica_sum(): arrived = lax.ppermute(values, 'replica', pairs)  108 us
    ppermute x28, waiting for transfers between devices, replica_sum(): arrived = lax.ppermute(piece(values, 1 - side, dim, size), 'replica', pairs)  90 us
    ppermute x28, starting transfers between devices, replica_sum(): arrived = lax.ppermute(piece(values, 1 - side, dim, size), 'replica', pairs)  35 us
    unnamed x109, local copies, waits for them, and re-layouts  22.7 us
    dot_general x3, matrix products, product(): return jnp.dot(left, right, preferred_element_type=jnp.float32)  22 us
    ppermute x28, starting transfers between devices, replica_sum(): arrived = lax.ppermute(values, 'replica', pairs)  22 us
    dot_general x6, matrix products, left_inner(): lax.dot_general(left, right, (((0,), (0,)), ((), ())), preferred_element_...  20.6 us
    dot_general x6, matrix products, contract(): lax.dot_general(left, right, (((left_dim,), (right_dim,)), ((), ())), pre...  19.2 us
  transfers between devices with their start and end apart: 66, of which 43 were waited for; matrix products, arithmetic and copies ran while one was open for 24% of the time, Pallas kernels for 2%

profile of v1, /device:TPU:0, one launch (start us, length us, event | category | flops | bytes accessed | tf_op | source)
XLA Modules:
  0.0 518.8 jit_solution(394333150353543285)
XLA Ops:
  18.4 8.4 %all-gather.7.cloned.1.call-done = bf16[960,1600]{1,0:T(8,128)(2,1)} async-done(((bf16[480,1600]{1,0:T(8,128)(2,1)}), bf16[960,1600]{1,0:T(8,128)(2,1)}) %all-gather.7.cloned.1.call-update) | async-done | bytes 3072016 | tf_op jit(solution)/shard_map/all_gather | solution.py:260
  35.1 11.1 %shard_map.203 = bf16[960,512]{1,0:T(8,128)(2,1)S(1)} custom-call(s32[512,1]{1,0:T(8,128)S(1)} %copy.74.seg_col, s32[1,512]{1,0:T(1,128)S(1)} %copy-done.1, bf16[960,512]{1,0:T(8,128)(2,1)S(1)} %bitcast.59, bf16[5,512,64]{2,1,0:T(8,128)(2,1)S(1)} %bitcast.61, bf16[320,512]{1,0:T(8,128)(2,1)S(1)} %slice.148.value), custom_call_target="tpu_custom_call" | custom-call | flops 4026531840 | bytes 3145728 | tf_op jit(solution)/shard_map/pallas_call | solution.py:153
  51.8 5.6 %all-gather.11.cloned.1.call-done = bf16[960,2560]{1,0:T(8,128)(2,1)} async-done(((bf16[960,1280]{1,0:T(8,128)(2,1)}), bf16[960,2560]{1,0:T(8,128)(2,1)}) %all-gather.11.cloned.1.call-update) | async-done | bytes 4915216 | tf_op jit(solution)/shard_map/all_gather | solution.py:264
  57.5 7.9 %fusion.51 = f32[512,2560]{1,0:T(8,128)} fusion(bf16[512,960]{0,1:T(8,128)(2,1)} %multiply_convert_fusion.3, bf16[960,2560]{1,0:T(8,128)(2,1)} %all-gather.11.cloned.1.call-done), kind=kOutput, calls=%fused_computation.245 | convolution fusion | flops 2516582400 | bytes 11141120 | tf_op jit(solution)/shard_map/dot_general | solution.py:21
  65.4 9.4 %all-gather.13.cloned.1.call-done = bf16[960,2560]{1,0:T(8,128)(2,1)} async-done(((bf16[960,1280]{1,0:T(8,128)(2,1)}), bf16[960,2560]{1,0:T(8,128)(2,1)}) %all-gather.13.cloned.1.call-update) | async-done | bytes 4915216 | tf_op jit(solution)/shard_map/all_gather | solution.py:265
  74.8 7.9 %fusion.52 = f32[512,2560]{1,0:T(8,128)} fusion(bf16[512,960]{0,1:T(8,128)(2,1)} %multiply_convert_fusion.3, bf16[960,2560]{1,0:T(8,128)(2,1)} %all-gather.13.cloned.1.call-done), kind=kOutput, calls=%fused_computation.246 | convolution fusion | flops 2516582400 | bytes 11141120 | tf_op jit(solution)/shard_map/dot_general | solution.py:21
  82.7 9.4 %all-gather.15.cloned.1.call-done = bf16[2560,960]{0,1:T(8,128)(2,1)} async-done(((bf16[1280,960]{0,1:T(8,128)(2,1)}), bf16[2560,960]{0,1:T(8,128)(2,1)}) %all-gather.15.cloned.1.call-update) | async-done | bytes 4915216 | tf_op jit(solution)/shard_map/all_gather | solution.py:266
  92.1 10.7 %multiply_convert_fusion = (bf16[512,2560]{1,0:T(8,128)(2,1)S(1)}, bf16[512,2560]{1,0:T(8,128)(2,1)S(1)}, bf16[512,2560]{1,0:T(8,128)(2,1)}) fusion(f32[512,2560]{1,0:T(8,128)} %fusion.51, f32[512,2560]{1,0:T(8,128)} %fusion.52, bf16[512,960]{0,1:T(8,128)(2,1)} %param.14, bf16[2560,960]{0,1:T(8,128)(2,1)} %all-gather.15.cloned.1.call-done), kind=kOutput, calls=%fused_computation.2 | convolution fusion | flops 2537553920 | bytes 24248320 | tf_op jit(solution)/shard_map/dot_general | solution.py:31
  119.5 17.7 %shard_map.204 = (f32[960,512]{1,0:T(8,128)S(1)}, f32[320,512]{1,0:T(8,128)S(1)}, f32[320,512]{1,0:T(8,128)S(1)}) custom-call(s32[512,1]{1,0:T(8,128)S(1)} %copy.74.seg_col, s32[1,512]{1,0:T(1,128)S(1)} %copy-done.1, bf16[960,512]{1,0:T(8,128)(2,1)S(1)} %bitcast.60, bf16[320,512]{1,0:T(8,128)(2,1)S(1)} %bitcast.58, bf16[5,512,64]{2,1,0:T(8,128)(2,1)S(1)} %bitcast.62, ...), custom_call_target="tpu_custom_call" | custom-call | flops 10066329600 | bytes 8388608 | tf_op jit(solution)/shard_map/pallas_call | solution.py:170
  163.2 6.2 %add_convert_fusion.5 = bf16[512,960]{0,1:T(8,128)(2,1)} fusion(f32[512,960]{0,1:T(8,128)S(1)} %copy-done.11, bf16[512,2560]{1,0:T(8,128)(2,1)S(1)} %copy-done.39, bf16[2560,960]{0,1:T(8,128)(2,1)} %all-gather.15.cloned.1.call-done), kind=kOutput, calls=%fused_computation.38 | convolution fusion | flops 2517565440 | bytes 10485760 | tf_op jit(solution)/shard_map/dot_general | solution.py:21
  205.2 9.3 %collective-permute-done.29 = bf16[32,960]{0,1:T(8,128)(2,1)S(1)} collective-permute-done((bf16[32,960]{0,1:T(8,128)(2,1)S(1)}, bf16[32,960]{0,1:T(8,128)(2,1)S(1)}, u32[]{:S(2)}, u32[]{:S(2)}) %collective-permute-start.29) | collective-permute-done | bytes 61472 | tf_op jit(solution)/shard_map/ppermute | solution.py:216
  222.0 12.2 %collective-permute-done.30 = bf16[32,960]{0,1:T(8,128)(2,1)S(1)} collective-permute-done((bf16[32,960]{0,1:T(8,128)(2,1)S(1)}, bf16[32,960]{0,1:T(8,128)(2,1)S(1)}, u32[]{:S(2)}, u32[]{:S(2)}) %collective-permute-start.30) | collective-permute-done | bytes 61472 | tf_op jit(solution)/shard_map/ppermute | solution.py:220
  236.6 6.5 %collective-permute-done.31 = bf16[64,960]{0,1:T(8,128)(2,1)S(1)} collective-permute-done((bf16[64,960]{0,1:T(8,128)(2,1)S(1)}, bf16[64,960]{0,1:T(8,128)(2,1)S(1)}, u32[]{:S(2)}, u32[]{:S(2)}) %collective-permute-start.31) | collective-permute-done | bytes 122912 | tf_op jit(solution)/shard_map/ppermute | solution.py:220
  264.6 6.9 %collective-permute-done.4 = bf16[32,512]{0,1:T(8,128)(2,1)S(1)} collective-permute-done((bf16[32,512]{0,1:T(8,128)(2,1)S(1)}, bf16[32,512]{0,1:T(8,128)(2,1)S(1)}, u32[]{:S(2)}, u32[]{:S(2)}) %collective-permute-start.4) | collective-permute-done | bytes 32800 | tf_op jit(solution)/shard_map/ppermute | solution.py:216
  271.6 6.6 %collective-permute-done.12 = bf16[32,512]{0,1:T(8,128)(2,1)S(1)} collective-permute-done((bf16[32,512]{0,1:T(8,128)(2,1)S(1)}, bf16[32,512]{0,1:T(8,128)(2,1)S(1)}, u32[]{:S(2)}, u32[]{:S(2)}) %collective-permute-start.12) | collective-permute-done | bytes 32800 | tf_op jit(solution)/shard_map/ppermute | solution.py:216
  283.6 5.8 %collective-permute-done.5 = bf16[32,512]{0,1:T(8,128)(2,1)S(1)} collective-permute-done((bf16[32,512]{0,1:T(8,128)(2,1)S(1)}, bf16[32,512]{0,1:T(8,128)(2,1)S(1)}, u32[]{:S(2)}, u32[]{:S(2)}) %collective-permute-start.5) | collective-permute-done | bytes 32800 | tf_op jit(solution)/shard_map/ppermute | solution.py:220
  289.5 7.2 %collective-permute-done.13 = bf16[32,512]{0,1:T(8,128)(2,1)S(1)} collective-permute-done((bf16[32,512]{0,1:T(8,128)(2,1)S(1)}, bf16[32,512]{0,1:T(8,128)(2,1)S(1)}, u32[]{:S(2)}, u32[]{:S(2)}) %collective-permute-start.13) | collective-permute-done | bytes 32800 | tf_op jit(solution)/shard_map/ppermute | solution.py:220
  296.9 7.1 %collective-permute-done.20 = bf16[32,576]{0,1:T(8,128)(2,1)S(1)} collective-permute-done((bf16[32,576]{0,1:T(8,128)(2,1)S(1)}, bf16[32,576]{0,1:T(8,128)(2,1)S(1)}, u32[]{:S(2)}, u32[]{:S(2)}) %collective-permute-start.20) | collective-permute-done | bytes 36896 | tf_op jit(solution)/shard_map/ppermute | solution.py:216
  315.1 6.5 %collective-permute-done.21 = bf16[32,576]{0,1:T(8,128)(2,1)S(1)} collective-permute-done((bf16[32,576]{0,1:T(8,128)(2,1)S(1)}, bf16[32,576]{0,1:T(8,128)(2,1)S(1)}, u32[]{:S(2)}, u32[]{:S(2)}) %collective-permute-start.21) | collective-permute-done | bytes 36896 | tf_op jit(solution)/shard_map/ppermute | solution.py:220
  376.5 5.6 %collective-permute-done.44 = bf16[480,1280]{1,0:T(8,128)(2,1)} collective-permute-done((bf16[480,1280]{1,0:T(8,128)(2,1)}, bf16[480,1280]{1,0:T(8,128)(2,1)}, u32[]{:S(2)}, u32[]{:S(2)}) %collective-permute-start.44) | collective-permute-done | bytes 1228832 | tf_op jit(solution)/shard_map/ppermute | solution.py:216
  418.1 7.4 %collective-permute-done.47 = bf16[120,640]{1,0:T(8,128)(2,1)S(1)} collective-permute-done((bf16[120,640]{1,0:T(8,128)(2,1)S(1)}, bf16[120,640]{1,0:T(8,128)(2,1)S(1)}, u32[]{:S(2)}, u32[]{:S(2)}) %collective-permute-start.47) | collective-permute-done | bytes 153632 | tf_op jit(solution)/shard_map/ppermute | solution.py:216
  449.4 8.6 %collective-permute-done.41 = bf16[240,1280]{1,0:T(8,128)(2,1)S(1)} collective-permute-done((bf16[240,1280]{1,0:T(8,128)(2,1)S(1)}, bf16[240,1280]{1,0:T(8,128)(2,1)S(1)}, u32[]{:S(2)}, u32[]{:S(2)}) %collective-permute-start.41) | collective-permute-done | bytes 614432 | tf_op jit(solution)/shard_map/ppermute | solution.py:220
  467.6 20.1 %collective-permute-done.59 = bf16[320,960]{1,0:T(8,128)(2,1)} collective-permute-done((bf16[320,960]{1,0:T(8,128)(2,1)}, bf16[320,960]{1,0:T(8,128)(2,1)}, u32[]{:S(2)}, u32[]{:S(2)}) %collective-permute-start.59) | collective-permute-done | bytes 614432 | tf_op jit(solution)/shard_map/ppermute | solution.py:220
  500.8 7.9 %collective-permute-done.60 = bf16[640,960]{0,1:T(8,128)(2,1)S(1)} collective-permute-done((bf16[640,960]{0,1:T(8,128)(2,1)S(1)}, bf16[640,960]{0,1:T(8,128)(2,1)S(1)}, u32[]{:S(2)}, u32[]{:S(2)}) %collective-permute-start.60) | collective-permute-done | bytes 1228832 | tf_op jit(solution)/shard_map/ppermute | solution.py:220
  (410 shorter events, 291.4 us)
Async XLA Ops:
  7.2 19.6 %all-gather.7.cloned.1.call-start = ((), (), s32[]{:S(2)}) async-start(), calls=%async_computation | async-start | bytes 4792320 | tf_op jit(solution)/shard_map/all_gather | solution.py:260
  11.8 34.5 %all-gather.9.cloned.1.call-start = ((), (), s32[]{:S(2)}) async-start(), calls=%async_computation.1 | async-start | bytes 2949120 | tf_op jit(solution)/shard_map/all_gather | solution.py:263
  12.5 44.9 %all-gather.11.cloned.1.call-start = ((), (), s32[]{:S(2)}) async-start(), calls=%async_computation.2 | async-start | bytes 7372800 | tf_op jit(solution)/shard_map/all_gather | solution.py:264
  13.3 61.5 %all-gather.13.cloned.1.call-start = ((), (), s32[]{:S(2)}) async-start(), calls=%async_computation.3 | async-start | bytes 7372800 | tf_op jit(solution)/shard_map/all_gather | solution.py:265
  13.9 78.2 %all-gather.15.cloned.1.call-start = ((), (), s32[]{:S(2)}) async-start(), calls=%async_computation.4 | async-start | bytes 7372800 | tf_op jit(solution)/shard_map/all_gather | solution.py:266
  155.5 34.5 %collective-permute-start = (bf16[512,1600]{0,1:T(8,128)(2,1)}, bf16[512,1600]{0,1:T(8,128)(2,1)}, u32[]{:S(2)}, u32[]{:S(2)}) collective-permute-start(bf16[512,1600]{0,1:T(8,128)(2,1)} %copy.87), channel_id=1, source_target_pairs={{0,1},{1,0},{2,3},{3,2},{4,5},{5,4},{6,7},{7,6},{8,9},{9,8},{10,11... | collective-permute-start | bytes 4915208 | tf_op jit(solution)/shard_map/ppermute | solution.py:233
  158.1 183.4 %collective-permute-start.34 = (bf16[960,1280]{1,0:T(8,128)(2,1)}, bf16[960,1280]{1,0:T(8,128)(2,1)}, u32[]{:S(2)}, u32[]{:S(2)}) collective-permute-start(bf16[960,1280]{1,0:T(8,128)(2,1)} %convolution_convert_fusion.2), channel_id=1, source_target_pairs={{0,1},{1,0},{2,3},{3,2},{4,5},{5,4},{6,7},{7,6},{8,9},{9,8},{10,11... | collective-permute-start | bytes 7372808 | tf_op jit(solution)/shard_map/ppermute | solution.py:233
  158.3 188.9 %collective-permute-start.43 = (bf16[960,1280]{1,0:T(8,128)(2,1)}, bf16[960,1280]{1,0:T(8,128)(2,1)}, u32[]{:S(2)}, u32[]{:S(2)}) collective-permute-start(bf16[960,1280]{1,0:T(8,128)(2,1)} %convolution_convert_fusion.1), channel_id=1, source_target_pairs={{0,1},{1,0},{2,3},{3,2},{4,5},{5,4},{6,7},{7,6},{8,9},{9,8},{10,11... | collective-permute-start | bytes 7372808 | tf_op jit(solution)/shard_map/ppermute | solution.py:233
  163.0 188.5 %collective-permute-start.52 = (bf16[1280,960]{0,1:T(8,128)(2,1)}, bf16[1280,960]{0,1:T(8,128)(2,1)}, u32[]{:S(2)}, u32[]{:S(2)}) collective-permute-start(bf16[1280,960]{0,1:T(8,128)(2,1)} %convolution_convert_fusion), channel_id=1, source_target_pairs={{0,1},{1,0},{2,3},{3,2},{4,5},{5,4},{6,7},{7,6},{8,9},{9,8},{10,11... | collective-permute-start | bytes 7372808 | tf_op jit(solution)/shard_map/ppermute | solution.py:233
  197.7 18.4 %collective-permute-start.1 = (bf16[256,512]{0,1:T(8,128)(2,1)S(1)}, bf16[256,512]{0,1:T(8,128)(2,1)S(1)}, u32[]{:S(2)}, u32[]{:S(2)}) collective-permute-start(bf16[256,512]{0,1:T(8,128)(2,1)S(1)} %constant_dynamic-slice_fusion.26), channel_id=1, source_target_pairs={{0,2},{2,0},{4,6},{6,4},{8,10},{10,8},{12,14},{14,12},{16,18},{18,... | collective-permute-start | bytes 786440 | tf_op jit(solution)/shard_map/ppermute | solution.py:216
  216.1 19.4 %collective-permute-start.17 = (bf16[256,576]{0,1:T(8,128)(2,1)S(1)}, bf16[256,576]{0,1:T(8,128)(2,1)S(1)}, u32[]{:S(2)}, u32[]{:S(2)}) collective-permute-start(bf16[256,576]{0,1:T(8,128)(2,1)S(1)} %constant_dynamic-slice_fusion.18), channel_id=1, source_target_pairs={{0,8},{2,10},{4,12},{6,14},{8,0},{10,2},{12,4},{14,6},{16,24},{18,... | collective-permute-start | bytes 884744 | tf_op jit(solution)/shard_map/ppermute | solution.py:216
  248.1 75.5 %collective-permute-start.32 = (bf16[128,960]{0,1:T(8,128)(2,1)S(1)}, bf16[128,960]{0,1:T(8,128)(2,1)S(1)}, u32[]{:S(2)}, u32[]{:S(2)}) collective-permute-start(bf16[128,960]{0,1:T(8,128)(2,1)S(1)} %pad_maximum_fusion.23), channel_id=1, source_target_pairs={{0,2},{2,0},{4,6},{6,4},{8,10},{10,8},{12,14},{14,12},{16,18},{18,... | collective-permute-start | bytes 737288 | tf_op jit(solution)/shard_map/ppermute | solution.py:220
  329.2 39.9 %collective-permute-start.33 = (bf16[256,960]{0,1:T(8,128)(2,1)S(1)}, bf16[256,960]{0,1:T(8,128)(2,1)}, u32[]{:S(2)}, u32[]{:S(2)}) collective-permute-start(bf16[256,960]{0,1:T(8,128)(2,1)S(1)} %pad_maximum_fusion.12), channel_id=1, source_target_pairs={{0,8},{2,10},{4,12},{6,14},{8,0},{10,2},{12,4},{14,6},{16,24},{18,... | collective-permute-start | bytes 1474568 | tf_op jit(solution)/shard_map/ppermute | solution.py:220
  339.0 19.5 %collective-permute-start.8 = (bf16[256,512]{0,1:T(8,128)(2,1)S(1)}, bf16[256,512]{0,1:T(8,128)(2,1)S(1)}, u32[]{:S(2)}, u32[]{:S(2)}) collective-permute-start(bf16[256,512]{0,1:T(8,128)(2,1)S(1)} %pad_maximum_fusion.19), channel_id=1, source_target_pairs={{0,2},{2,0},{4,6},{6,4},{8,10},{10,8},{12,14},{14,12},{16,18},{18,... | collective-permute-start | bytes 786440 | tf_op jit(solution)/shard_map/ppermute | solution.py:220
  341.5 17.9 %collective-permute-start.16 = (bf16[256,512]{0,1:T(8,128)(2,1)S(1)}, bf16[256,512]{0,1:T(8,128)(2,1)S(1)}, u32[]{:S(2)}, u32[]{:S(2)}) collective-permute-start(bf16[256,512]{0,1:T(8,128)(2,1)S(1)} %pad_maximum_fusion.20), channel_id=1, source_target_pairs={{0,4},{2,6},{4,0},{6,2},{8,12},{10,14},{12,8},{14,10},{16,20},{18,... | collective-permute-start | bytes 786440 | tf_op jit(solution)/shard_map/ppermute | solution.py:220
  347.9 18.8 %collective-permute-start.24 = (bf16[256,576]{0,1:T(8,128)(2,1)}, bf16[256,576]{0,1:T(8,128)(2,1)}, u32[]{:S(2)}, u32[]{:S(2)}) collective-permute-start(bf16[256,576]{0,1:T(8,128)(2,1)} %pad_maximum_fusion.18), channel_id=1, source_target_pairs={{0,8},{2,10},{4,12},{6,14},{8,0},{10,2},{12,4},{14,6},{16,24},{18,... | collective-permute-start | bytes 884744 | tf_op jit(solution)/shard_map/ppermute | solution.py:220
  351.6 20.8 %collective-permute-start.35 = (bf16[480,1280]{1,0:T(8,128)(2,1)}, bf16[480,1280]{1,0:T(8,128)(2,1)}, u32[]{:S(2)}, u32[]{:S(2)}) collective-permute-start(bf16[480,1280]{1,0:T(8,128)(2,1)} %constant_dynamic-slice_fusion.11), channel_id=1, source_target_pairs={{0,2},{2,0},{4,6},{6,4},{8,10},{10,8},{12,14},{14,12},{16,18},{18,... | collective-permute-start | bytes 3686408 | tf_op jit(solution)/shard_map/ppermute | solution.py:216
  358.5 23.6 %collective-permute-start.44 = (bf16[480,1280]{1,0:T(8,128)(2,1)}, bf16[480,1280]{1,0:T(8,128)(2,1)}, u32[]{:S(2)}, u32[]{:S(2)}) collective-permute-start(bf16[480,1280]{1,0:T(8,128)(2,1)} %constant_dynamic-slice_fusion.7), channel_id=1, source_target_pairs={{0,4},{2,6},{4,0},{6,2},{8,12},{10,14},{12,8},{14,10},{16,20},{18,... | collective-permute-start | bytes 3686408 | tf_op jit(solution)/shard_map/ppermute | solution.py:216
  359.5 26.8 %collective-permute-start.53 = (bf16[640,960]{0,1:T(8,128)(2,1)}, bf16[640,960]{0,1:T(8,128)(2,1)}, u32[]{:S(2)}, u32[]{:S(2)}) collective-permute-start(bf16[640,960]{0,1:T(8,128)(2,1)} %constant_dynamic-slice_fusion.3), channel_id=1, source_target_pairs={{0,8},{2,10},{4,12},{6,14},{8,0},{10,2},{12,4},{14,6},{16,24},{18,... | collective-permute-start | bytes 3686408 | tf_op jit(solution)/shard_map/ppermute | solution.py:216
  407.9 17.5 %collective-permute-start.47 = (bf16[120,640]{1,0:T(8,128)(2,1)S(1)}, bf16[120,640]{1,0:T(8,128)(2,1)S(1)}, u32[]{:S(2)}, u32[]{:S(2)}) collective-permute-start(bf16[120,640]{1,0:T(8,128)(2,1)S(1)} %constant_dynamic-slice_fusion.4), channel_id=1, source_target_pairs={{0,16},{2,18},{4,20},{6,22},{8,24},{10,26},{12,28},{14,30},{16,0},... | collective-permute-start | bytes 460808 | tf_op jit(solution)/shard_map/ppermute | solution.py:216
  459.4 32.6 %collective-permute-start.42 = (bf16[480,1280]{1,0:T(8,128)(2,1)}, bf16[480,1280]{1,0:T(8,128)(2,1)}, u32[]{:S(2)}, u32[]{:S(2)}) collective-permute-start(bf16[480,1280]{1,0:T(8,128)(2,1)} %pad_maximum_fusion.1), channel_id=1, source_target_pairs={{0,2},{2,0},{4,6},{6,4},{8,10},{10,8},{12,14},{14,12},{16,18},{18,... | collective-permute-start | bytes 3686408 | tf_op jit(solution)/shard_map/ppermute | solution.py:220
  462.3 25.4 %collective-permute-start.59 = (bf16[320,960]{1,0:T(8,128)(2,1)}, bf16[320,960]{1,0:T(8,128)(2,1)}, u32[]{:S(2)}, u32[]{:S(2)}) collective-permute-start(bf16[320,960]{1,0:T(8,128)(2,1)} %copy.80), channel_id=1, source_target_pairs={{0,2},{2,0},{4,6},{6,4},{8,10},{10,8},{12,14},{14,12},{16,18},{18,... | collective-permute-start | bytes 1843208 | tf_op jit(solution)/shard_map/ppermute | solution.py:220
  465.3 31.1 %collective-permute-start.51 = (bf16[480,1280]{1,0:T(8,128)(2,1)}, bf16[480,1280]{1,0:T(8,128)(2,1)}, u32[]{:S(2)}, u32[]{:S(2)}) collective-permute-start(bf16[480,1280]{1,0:T(8,128)(2,1)} %pad_maximum_fusion.2), channel_id=1, source_target_pairs={{0,4},{2,6},{4,0},{6,2},{8,12},{10,14},{12,8},{14,10},{16,20},{18,... | collective-permute-start | bytes 3686408 | tf_op jit(solution)/shard_map/ppermute | solution.py:220
  491.9 16.8 %collective-permute-start.60 = (bf16[640,960]{0,1:T(8,128)(2,1)S(1)}, bf16[640,960]{0,1:T(8,128)(2,1)S(1)}, u32[]{:S(2)}, u32[]{:S(2)}) collective-permute-start(bf16[640,960]{0,1:T(8,128)(2,1)S(1)} %pad_maximum_fusion.3), channel_id=1, source_target_pairs={{0,8},{2,10},{4,12},{6,14},{8,0},{10,2},{12,4},{14,6},{16,24},{18,... | collective-permute-start | bytes 3686408 | tf_op jit(solution)/shard_map/ppermute | solution.py:220
  (93 other events, 658.2 us)
Sparse Core Ops, SparseCore 0:
  11.9 14.8 all-gather.6
  28.4 11.5 all-gather.8
  41.5 15.8 all-gather.10
  58.8 15.8 all-gather.12
  76.2 15.8 all-gather.14

commit v2 on v1

--- a/solution.py
+++ b/solution.py
@@ -188,56 +188,35 @@
     return values.reshape(-1, HEAD_SIZE, values.shape[1]).transpose(0, 2, 1)
 
 
-def halving_dim(shape):
-    if shape[0] % 16 == 0:
-        return 0
-    if shape[1] % 256 == 0:
-        return 1
-    return 0 if shape[0] % 2 == 0 else 1
-
-
-def piece(values, which, dim, size):
-    return lax.dynamic_slice_in_dim(values, which * size, size, dim)
-
-
-def replica_sum(values, order, replicas):
-    levels = replicas.bit_length() - 1
-    if replicas != 1 << levels:
-        return lax.psum(values, "replica").astype(jnp.float32)
-    bits = [bit for bit in order if bit < levels]
-    bits += [bit for bit in range(levels) if bit not in bits]
-    index = lax.axis_index("replica")
-    taken = []
-    for bit in bits:
-        pairs = [(i, i ^ (1 << bit)) for i in range(replicas)]
-        dim = halving_dim(values.shape)
-        size = values.shape[dim] // 2
-        side = (index >> bit) & 1
-        arrived = lax.ppermute(piece(values, 1 - side, dim, size), "replica", pairs)
-        values = piece(values, side, dim, size) + arrived
-        taken.append((pairs, dim, side))
-    for pairs, dim, side in reversed(taken):
-        arrived = lax.ppermute(values, "replica", pairs)
-        low_side = side == 0
-        values = jnp.concatenate(
-            [jnp.where(low_side, values, arrived), jnp.where(low_side, arrived, values)], dim
+def gather_rows(values, shards):
+    if shards != 2:
+        return lax.all_gather(values, "shard", axis=0, tiled=True)
+    arrived = lax.ppermute(values, "shard", [(0, 1), (1, 0)])
+    first = lax.axis_index("shard") == 0
+    return jnp.concatenate(
+        [jnp.where(first, values, arrived), jnp.where(first, arrived, values)], 0
+    )
+
+
+def others(values, shards):
+    blocks = [values]
+    for step in range(1, shards):
+        pairs = [((i + step) % shards, i) for i in range(shards)]
+        blocks.append(lax.ppermute(values, "shard", pairs))
+    return blocks
+
+
+def returned(parts, shards):
+    total = parts[0]
+    for step in range(1, shards):
+        pairs = [(i, (i + step) % shards) for i in range(shards)]
+        total = total + lax.ppermute(parts[step].astype(jnp.bfloat16), "shard", pairs).astype(
+            jnp.float32
         )
-    return values.astype(jnp.float32)
-
-
-def shard_sum(make, dim, full, shards):
-    if shards == 2:
-        size = full // 2
-        side = lax.axis_index("shard")
-        sent = make(1 - side, size).astype(jnp.bfloat16)
-        arrived = lax.ppermute(sent, "shard", [(0, 1), (1, 0)])
-        return (make(side, size) + arrived.astype(jnp.float32)).astype(jnp.bfloat16)
-    whole = make(0, full).astype(jnp.bfloat16)
-    return lax.psum_scatter(whole, "shard", scatter_dimension=dim, tiled=True)
+    return total.astype(jnp.bfloat16)
 
 
 def per_device(
-    replicas,
     shards,
     layer_input,
     segment_ids,
@@ -254,19 +233,18 @@
 ):
     segment = segment_ids.reshape(-1)
     features = layer_input.shape[1]
-    hidden = gate_weight.shape[1] * shards
     query_size, key_size = query_weight.shape[1], key_weight.shape[1]
-    gains = lax.all_gather(jnp.stack([attn_gain, ffn_gain]), "shard", axis=1, tiled=True)
-    projections = lax.all_gather(
-        jnp.concatenate([query_weight, key_weight, value_weight], 1), "shard", axis=0, tiled=True
-    )
-    output_w = lax.all_gather(output_weight, "shard", axis=0, tiled=True)
-    gate_w = lax.all_gather(gate_weight, "shard", axis=1, tiled=True)
-    up_w = lax.all_gather(up_weight, "shard", axis=1, tiled=True)
-    down_w = lax.all_gather(down_weight, "shard", axis=0, tiled=True)
-
-    gain_one = gains[0].astype(jnp.float32)
-    gain_two = gains[1].astype(jnp.float32)
+    gains = gather_rows(jnp.stack([attn_gain, ffn_gain], 1), shards)
+    projections = gather_rows(
+        jnp.concatenate([query_weight, key_weight, value_weight], 1), shards
+    )
+    output_w = gather_rows(output_weight, shards)
+    gate_blocks = others(gate_weight, shards)
+    up_blocks = others(up_weight, shards)
+    down_blocks = others(down_weight, shards)
+
+    gain_one = gains[:, 0].astype(jnp.float32)
+    gain_two = gains[:, 1].astype(jnp.float32)
     start_input = layer_input.astype(jnp.float32)
     normed_one, inverse_one = normalize(start_input)
     hidden_one = (normed_one * gain_one).astype(jnp.bfloat16)
@@ -281,40 +259,33 @@
     normed_two, inverse_two = normalize(middle)
     hidden_two = (normed_two * gain_two).astype(jnp.bfloat16)
 
-    gate_value = product(hidden_two, gate_w)
-    up_value = product(hidden_two, up_w)
-    sigma = jax.nn.sigmoid(gate_value)
-    grad_activ = right_inner(upstream_grad, down_w)
-    activ_low = (gate_value * sigma * up_value).astype(jnp.bfloat16)
-    grad_gate = (grad_activ * up_value * sigma * (1.0 + gate_value * (1.0 - sigma))).astype(
-        jnp.bfloat16
-    )
-    grad_up = (grad_activ * gate_value * sigma).astype(jnp.bfloat16)
-
-    gate_grad = shard_sum(
-        lambda which, size: left_inner(hidden_two, piece(grad_gate, which, 1, size)),
-        1,
-        hidden,
-        shards,
-    )
-    gate_grad = replica_sum(gate_grad, ORDERS[0], replicas)
-    up_grad = shard_sum(
-        lambda which, size: left_inner(hidden_two, piece(grad_up, which, 1, size)),
-        1,
-        hidden,
-        shards,
-    )
-    up_grad = replica_sum(up_grad, ORDERS[1], replicas)
-    down_grad = shard_sum(
-        lambda which, size: left_inner(piece(activ_low, which, 1, size), upstream_grad),
-        0,
-        hidden,
-        shards,
-    )
-    down_grad = replica_sum(down_grad, ORDERS[2], replicas)
-
-    layer_output = (middle + product(activ_low, down_w)).astype(jnp.bfloat16)
-    grad_hidden_two = right_inner(grad_gate, gate_w) + right_inner(grad_up, up_w)
+    grad_hidden_two = jnp.zeros_like(middle)
+    down_out = middle
+    gate_parts, up_parts, down_parts = [], [], []
+    for gate_w, up_w, down_w in zip(gate_blocks, up_blocks, down_blocks):
+        gate_value = product(hidden_two, gate_w)
+        up_value = product(hidden_two, up_w)
+        sigma = jax.nn.sigmoid(gate_value)
+        grad_activ = right_inner(upstream_grad, down_w)
+        activ_low = (gate_value * sigma * up_value).astype(jnp.bfloat16)
+        grad_gate = (grad_activ * up_value * sigma * (1.0 + gate_value * (1.0 - sigma))).astype(
+            jnp.bfloat16
+        )
+        grad_up = (grad_activ * gate_value * sigma).astype(jnp.bfloat16)
+        gate_parts.append(left_inner(hidden_two, grad_gate))
+        up_parts.append(left_inner(hidden_two, grad_up))
+        down_parts.append(left_inner(activ_low, upstream_grad))
+        down_out = down_out + product(activ_low, down_w)
+        grad_hidden_two = (
+            grad_hidden_two + right_inner(grad_gate, gate_w) + right_inner(grad_up, up_w)
+        )
+    layer_output = down_out.astype(jnp.bfloat16)
+    ffn_own = (
+        returned(gate_parts, shards),
+        returned(up_parts, shards),
+        returned(down_parts, shards),
+    )
+    ffn_sums = lax.psum(ffn_own, "replica")
     gain_two_part = jnp.sum(grad_hidden_two * normed_two, 0)
     grad_middle = upstream_grad.astype(jnp.float32) + norm_backward(
         grad_hidden_two * gain_two, normed_two, inverse_two
@@ -322,16 +293,11 @@
     grad_middle_low = grad_middle.astype(jnp.bfloat16)
 
     rows = features // shards
-    padded = -(-(rows + 1) // 128) * 128
+    padded = -(-(rows + 1) // 16) * 16
 
     output_part = contract(mixed, grad_middle_low, 1, 0)
-    output_grad = shard_sum(
-        lambda which, size: piece(output_part, which, 0, size), 0, query_size, shards
-    )
-    output_grad = jnp.pad(output_grad, ((0, padded - output_grad.shape[0]), (0, 0)))
-    output_grad = replica_sum(output_grad, ORDERS[2], replicas)[: query_size // shards]
-
     grad_mixed = contract(output_w, grad_middle_low, 1, 1).astype(jnp.bfloat16)
+    grad_mixed, _ = lax.optimization_barrier((grad_mixed, ffn_own))
     grad_query, grad_key, grad_value = attention_backward(
         segment, query, key, key_rows, value_rows, grad_mixed
     )
@@ -347,27 +313,31 @@
     gain_one_part = jnp.sum(grad_hidden_one * normed_one, 0)
     input_grad = grad_middle + norm_backward(grad_hidden_one * gain_one, normed_one, inverse_one)
 
-    projection_part = contract(hidden_one, grad_projected, 0, 1)
+    projection_part = jnp.concatenate(
+        [contract(hidden_one, grad_projected, 0, 1), output_part], 1
+    ).astype(jnp.bfloat16)
     width = projection_part.shape[1]
     gain_parts = jnp.stack([gain_one_part, gain_two_part]).reshape(2, shards, rows)
     gain_rows = gain_parts.transpose(1, 0, 2).reshape(shards, 1, 2 * rows)
     gain_rows = jnp.pad(gain_rows, ((0, 0), (0, padded - rows - 1), (0, width - 2 * rows)))
-    packed = jnp.concatenate([projection_part.reshape(shards, rows, width), gain_rows], 1)
-    packed = packed.reshape(shards * padded, width)
-    packed = shard_sum(
-        lambda which, size: piece(packed, which, 0, size), 0, shards * padded, shards
-    )
-    cuts = [0, width // 384 * 128, width // 384 * 256, width]
     packed = jnp.concatenate(
-        [
-            replica_sum(packed[:, cuts[i] : cuts[i + 1]], ORDERS[i], replicas)
-            for i in range(3)
-        ],
-        1,
-    )
-    query_grad = packed[:rows, :query_size]
-    key_grad = packed[:rows, query_size : query_size + key_size]
-    value_grad = packed[:rows, query_size + key_size :]
+        [projection_part.reshape(shards, rows, width), gain_rows.astype(jnp.bfloat16)], 1
+    )
+    side = lax.axis_index("shard")
+    packed = [
+        lax.dynamic_index_in_dim(packed, lax.rem(side + step, shards), 0, keepdims=False).astype(
+            jnp.float32
+        )
+        for step in range(shards)
+    ]
+    packed, ffn_sums = lax.optimization_barrier((returned(packed, shards), ffn_sums))
+    packed = lax.psum(packed, "replica").astype(jnp.float32)
+    gate_grad, up_grad, down_grad = [total.astype(jnp.float32) for total in ffn_sums]
+    ends = [query_size, query_size + key_size, query_size + 2 * key_size]
+    query_grad = packed[:rows, : ends[0]]
+    key_grad = packed[:rows, ends[0] : ends[1]]
+    value_grad = packed[:rows, ends[1] : ends[2]]
+    output_grad = packed[:rows, ends[2] :]
     gain_one_grad = packed[rows, :rows]
     gain_two_grad = packed[rows, rows : 2 * rows]
     return (
@@ -385,9 +355,6 @@
     )
 
 
-ORDERS = ((0, 1, 2, 3), (1, 2, 0, 3), (2, 0, 1, 3))
-
-
 def solution(mesh):
     placed = (
         P(("replica", "shard"), None),
@@ -404,7 +371,7 @@
         P("shard", None),
     )
     return jax.shard_map(
-        functools.partial(per_device, mesh.shape["replica"], mesh.shape["shard"]),
+        functools.partial(per_device, mesh.shape["shard"]),
         mesh=mesh,
         in_specs=placed,
         out_specs=(

time: 524 us -> 489 us (0.933)
  waiting for transfers between devices: 233 us -> 321 us
  starting transfers between devices: 58.5 us -> 3.05 us
  other arithmetic: 55.7 us -> 27.1 us
  local copies, waits for them, and re-layouts: 47.1 us -> 24.9 us
  matrix products: 78.3 us -> 63.9 us
    psum x0 -> x2, waiting for transfers between devices: none -> 314 us  [the longest x1 193 us: per_device(): ffn_sums = lax.psum(ffn_own, 'replica')]
    ppermute x61 -> x10, waiting for transfers between devices: 198 us -> 7.15 us  [the longest x4 4.87 us: returned(): lax.ppermute(parts[step].astype(jnp.bfloat16), 'shard', pairs)]
    ppermute x61 -> x10, starting transfers between devices: 58.3 us -> 2.97 us  [the longest x4 1.22 us: returned(): lax.ppermute(parts[step].astype(jnp.bfloat16), 'shard', pairs)]
    all_gather x5 -> x0, waiting for transfers between devices: 32.9 us -> none  [the longest x1 9.43 us: per_device(): down_w = lax.all_gather(down_weight, 'shard', axis=0, tiled=True)]
    dynamic_slice x31 -> x0, local copies, waits for them, and re-layouts: 13.4 us -> none  [piece(): return lax.dynamic_slice_in_dim(values, which * size, size, dim)]
    add x28 -> x0, other arithmetic: 10.4 us -> none  [replica_sum(): values = piece(values, side, dim, size) + arrived]
    unnamed x109 -> x74, local copies, waits for them, and re-layouts: 22.7 us -> 14 us
    select_n x28 -> x3, other arithmetic: 12.1 us -> 4.75 us  [gather_rows(): jnp.where(first, values, arrived)]
  transfers between devices with their start and end apart: 66 -> 12, of which waited for: 43 -> 5; matrix products, arithmetic and copies ran while one was open for 24% -> 18% of each run, Pallas kernels for 2% -> 6%
where the time goes in v2:
time: 489 us; the launch traced here: 483 us
  waiting for transfers between devices  321 us (66%)
  matrix products  63.9 us (13%)
  Pallas kernels  28.3 us (6%)
  other arithmetic  27.1 us (6%)
  local copies, waits for them, and re-layouts  24.9 us (5%)
  between operations  14.9 us (3%)
    psum x1, waiting for transfers between devices, per_device(): ffn_sums = lax.psum(ffn_own, 'replica')  193 us
    psum x1, waiting for transfers between devices, per_device(): packed = lax.psum(packed, 'replica').astype(jnp.float32)  121 us
    dot_general x6, matrix products, product(): return jnp.dot(left, right, preferred_element_type=jnp.float32)  18.3 us
    pallas_call x1, Pallas kernels, attention_backward(): pl.pallas_call(backward_kernel, grid=(KEY_VALUE_HEADS,), out_shape=(jax.S...  17.2 us
    dot_general x6, matrix products, contract(): lax.dot_general(left, right, (((left_dim,), (right_dim,)), ((), ())), pre...  16.4 us
    dot_general x6, matrix products, right_inner(): lax.dot_general(left, right, (((1,), (1,)), ((), ())), preferred_element_...  15.8 us
    unnamed x74, local copies, waits for them, and re-layouts  14 us
    dot_general x6, matrix products, left_inner(): lax.dot_general(left, right, (((0,), (0,)), ((), ())), preferred_element_...  13.4 us
  transfers between devices with their start and end apart: 12, of which 5 were waited for; matrix products, arithmetic and copies ran while one was open for 18% of the time, Pallas kernels for 6%

profile of v2, /device:TPU:0, one launch (start us, length us, event | category | flops | bytes accessed | tf_op | source)
XLA Modules:
  0.0 483.2 jit_solution(9457613652312282057)
XLA Ops:
  18.3 2.9 broadcast_select_fusion.3
  26.4 11.1 %shard_map.203 = bf16[960,512]{1,0:T(8,128)(2,1)S(1)} custom-call(s32[512,1]{1,0:T(8,128)S(1)} %copy.48.seg_col, s32[1,512]{1,0:T(1,128)S(1)} %copy-done, bf16[960,512]{1,0:T(8,128)(2,1)S(1)} %bitcast.71, bf16[5,512,64]{2,1,0:T(8,128)(2,1)S(1)} %bitcast.73, bf16[320,512]{1,0:T(8,128)(2,1)S(1)} %slice.120.value), custom_call_target="tpu_custom_call" | custom-call | flops 4026531840 | bytes 3145728 | tf_op jit(solution)/shard_map/pallas_call | solution.py:153
  46.4 2.7 multiply_convert_fusion.2
  52.1 3.3 fusion.37
  55.3 3.3 fusion.34
  58.6 4.6 multiply_convert_fusion.1
  68.7 3.3 fusion.38
  72.0 3.7 multiply_reduce_fusion
  79.4 2.9 add_convert_fusion.2
  82.3 2.9 add_convert_fusion.1
  85.1 3.3 add_convert_fusion
  88.5 4.3 convolution_convert_fusion.4
  94.1 17.2 %shard_map.204 = (f32[960,512]{1,0:T(8,128)S(1)}, f32[320,512]{1,0:T(8,128)S(1)}, f32[320,512]{1,0:T(8,128)S(1)}) custom-call(s32[512,1]{1,0:T(8,128)S(1)} %copy.48.seg_col, s32[1,512]{1,0:T(1,128)S(1)} %copy-done, bf16[960,512]{1,0:T(8,128)(2,1)S(1)} %bitcast.72, bf16[320,512]{1,0:T(8,128)(2,1)S(1)} %bitcast.70, bf16[5,512,64]{2,1,0:T(8,128)(2,1)S(1)} %bitcast.74, ...), custom_call_target="tpu_custom_call" | custom-call | flops 10066329600 | bytes 8388608 | tf_op jit(solution)/shard_map/pallas_call | solution.py:170
  113.8 3.4 fusion.14
  119.4 3.8 fusion.1
  126.4 4.9 %collective-permute-done.9 = bf16[496,2560]{1,0:T(8,128)(2,1)S(1)} collective-permute-done((bf16[496,2560]{1,0:T(8,128)(2,1)}, bf16[496,2560]{1,0:T(8,128)(2,1)S(1)}, u32[]{:S(2)}, u32[]{:S(2)}) %collective-permute-start.9) | collective-permute-done | bytes 2539552 | tf_op jit(solution)/shard_map/ppermute | solution.py:213
  131.3 4.1 fusion.2
  135.4 192.6 %all-reduce.7.cloned.1.call-done = (bf16[960,1280]{1,0:T(8,128)(2,1)}, bf16[960,1280]{1,0:T(8,128)(2,1)}, bf16[1280,960]{0,1:T(8,128)(2,1)}) async-done(((bf16[960,1280]{1,0:T(8,128)(2,1)}, bf16[960,1280]{1,0:T(8,128)(2,1)}, bf16[1280,960]{0,1:T(8,128)(2,1)}), (bf16[960,1280]{1,0:T(8,128)(2,1)}, bf16[960,1280]{1,0:T(8,128)(2,1)}, bf16[1280,960]{0,1:T(8,128)(2,1)})) %all-reduce.7.cloned.1.call-update) | async-done | bytes 7372816 | tf_op jit(solution)/shard_map/psum | solution.py:288
  328.1 2.9 fusion.33
  331.0 4.4 add_convert_fusion.3
  337.7 2.7 convert_element_type.177
  341.0 2.6 convert_element_type.178
  343.6 2.6 convert_element_type.179
  346.2 121.2 %all-reduce.5.cloned.1.call-done = bf16[496,2560]{1,0:T(8,128)(2,1)} async-done(((bf16[496,2560]{1,0:T(8,128)(2,1)}), bf16[496,2560]{1,0:T(8,128)(2,1)}) %all-reduce.5.cloned.1.call-update) | async-done | bytes 2539536 | tf_op jit(solution)/shard_map/psum | solution.py:334
  (152 shorter events, 57.6 us)
Async XLA Ops:
  7.2 320.8 %all-reduce.7.cloned.1.call-start = ((), (), s32[]{:S(2)}) async-start(), calls=%async_computation.1 | async-start | bytes 14745600 | tf_op jit(solution)/shard_map/psum | solution.py:288
  8.4 5.1 %copy-start.28 = (bf16[480]{0:T(512)(128)(2,1)S(1)}, bf16[480]{0:T(512)(128)(2,1)}, u32[]{:S(2)}) copy-start(bf16[480]{0:T(512)(128)(2,1)} %param.20) | copy-start | bytes 2884
  8.5 5.1 %copy-start.29 = (bf16[480]{0:T(512)(128)(2,1)S(1)}, bf16[480]{0:T(512)(128)(2,1)}, u32[]{:S(2)}) copy-start(bf16[480]{0:T(512)(128)(2,1)} %param.15) | copy-start | bytes 2884
  8.5 6.2 %copy-start = (s32[1,512]{1,0:T(1,128)S(1)}, s32[1,512]{1,0:T(1,128)}, u32[]{:S(2)}) copy-start(s32[1,512]{1,0:T(1,128)} %seg_row.3) | copy-start | bytes 6148
  8.5 6.6 %copy-start.10 = (bf16[512,960]{0,1:T(8,128)(2,1)S(1)}, bf16[512,960]{0,1:T(8,128)(2,1)}, u32[]{:S(2)}) copy-start(bf16[512,960]{0,1:T(8,128)(2,1)} %param.12) | copy-start | bytes 2949124
  13.0 8.2 %collective-permute-start = (bf16[480,1600]{1,0:T(8,128)(2,1)S(1)}, bf16[480,1600]{1,0:T(8,128)(2,1)}, u32[]{:S(2)}, u32[]{:S(2)}) collective-permute-start(bf16[480,1600]{1,0:T(8,128)(2,1)S(1)} %concatenate.29), channel_id=1, source_target_pairs={{0,1},{1,0},{2,3},{3,2},{4,5},{5,4},{6,7},{7,6},{8,9},{9,8},{10,11... | collective-permute-start | bytes 4608008 | tf_op jit(solution)/shard_map/ppermute | solution.py:194
  13.6 2.9 collective-permute-start.1
  13.7 4.7 collective-permute-start.2
  14.1 37.9 %collective-permute-start.5 = (bf16[1280,960]{0,1:T(8,128)(2,1)}, bf16[1280,960]{0,1:T(8,128)(2,1)}, u32[]{:S(2)}, u32[]{:S(2)}) collective-permute-start(bf16[1280,960]{0,1:T(8,128)(2,1)} %param.23), channel_id=1, source_target_pairs={{1,0},{0,1},{3,2},{2,3},{5,4},{4,5},{7,6},{6,7},{9,8},{8,9},{11,10... | collective-permute-start | bytes 7372808 | tf_op jit(solution)/shard_map/ppermute | solution.py:205
  14.2 41.1 %collective-permute-start.4 = (bf16[960,1280]{1,0:T(8,128)(2,1)}, bf16[960,1280]{1,0:T(8,128)(2,1)}, u32[]{:S(2)}, u32[]{:S(2)}) collective-permute-start(bf16[960,1280]{1,0:T(8,128)(2,1)} %param.22), channel_id=1, source_target_pairs={{1,0},{0,1},{3,2},{2,3},{5,4},{4,5},{7,6},{6,7},{9,8},{8,9},{11,10... | collective-permute-start | bytes 7372808 | tf_op jit(solution)/shard_map/ppermute | solution.py:205
  16.5 42.1 %collective-permute-start.3 = (bf16[960,1280]{1,0:T(8,128)(2,1)}, bf16[960,1280]{1,0:T(8,128)(2,1)}, u32[]{:S(2)}, u32[]{:S(2)}) collective-permute-start(bf16[960,1280]{1,0:T(8,128)(2,1)} %param.21), channel_id=1, source_target_pairs={{1,0},{0,1},{3,2},{2,3},{5,4},{4,5},{7,6},{6,7},{9,8},{8,9},{11,10... | collective-permute-start | bytes 7372808 | tf_op jit(solution)/shard_map/ppermute | solution.py:205
  26.4 11.2 %copy-start.11 = (bf16[512,960]{0,1:T(8,128)(2,1)S(1)}, bf16[512,960]{0,1:T(8,128)(2,1)}, u32[]{:S(2)}) copy-start(bf16[512,960]{0,1:T(8,128)(2,1)} %param.12) | copy-start | bytes 2949124
  26.4 11.2 %copy-start.24 = (bf16[480,960]{1,0:T(8,128)(2,1)S(1)}, bf16[480,960]{1,0:T(8,128)(2,1)}, u32[]{:S(2)}) copy-start(bf16[480,960]{1,0:T(8,128)(2,1)} %get-tuple-element.86) | copy-start | bytes 2764804
  26.4 11.2 %copy-start.26 = (bf16[480,960]{1,0:T(8,128)(2,1)S(1)}, bf16[480,960]{1,0:T(8,128)(2,1)}, u32[]{:S(2)}) copy-start(bf16[480,960]{1,0:T(8,128)(2,1)} %get-tuple-element.87) | copy-start | bytes 2764804
  49.1 36.0 %copy-start.34 = (bf16[512,1280]{1,0:T(8,128)(2,1)}, bf16[512,1280]{1,0:T(8,128)(2,1)S(1)}, u32[]{:S(2)}) copy-start(bf16[512,1280]{1,0:T(8,128)(2,1)S(1)} %get-tuple-element.70) | copy-start | bytes 3932164
  64.7 14.7 %collective-permute-start.6 = (bf16[960,1280]{1,0:T(8,128)(2,1)S(1)}, bf16[960,1280]{1,0:T(8,128)(2,1)S(1)}, u32[]{:S(2)}, u32[]{:S(2)}) collective-permute-start(bf16[960,1280]{1,0:T(8,128)(2,1)S(1)} %convolution_convert_fusion.2), channel_id=1, source_target_pairs={{0,1},{1,0},{2,3},{3,2},{4,5},{5,4},{6,7},{7,6},{8,9},{9,8},{10,11... | collective-permute-start | bytes 7372808 | tf_op jit(solution)/shard_map/ppermute | solution.py:213
  66.6 15.7 %collective-permute-start.7 = (bf16[960,1280]{1,0:T(8,128)(2,1)S(1)}, bf16[960,1280]{1,0:T(8,128)(2,1)S(1)}, u32[]{:S(2)}, u32[]{:S(2)}) collective-permute-start(bf16[960,1280]{1,0:T(8,128)(2,1)S(1)} %convolution_convert_fusion.1), channel_id=1, source_target_pairs={{0,1},{1,0},{2,3},{3,2},{4,5},{5,4},{6,7},{7,6},{8,9},{9,8},{10,11... | collective-permute-start | bytes 7372808 | tf_op jit(solution)/shard_map/ppermute | solution.py:213
  68.2 3.8 copy-start.4
  68.3 16.9 %collective-permute-start.8 = (bf16[1280,960]{0,1:T(8,128)(2,1)S(1)}, bf16[1280,960]{0,1:T(8,128)(2,1)S(1)}, u32[]{:S(2)}, u32[]{:S(2)}) collective-permute-start(bf16[1280,960]{0,1:T(8,128)(2,1)S(1)} %convolution_convert_fusion), channel_id=1, source_target_pairs={{0,1},{1,0},{2,3},{3,2},{4,5},{5,4},{6,7},{7,6},{8,9},{9,8},{10,11... | collective-permute-start | bytes 7372808 | tf_op jit(solution)/shard_map/ppermute | solution.py:213
  88.5 379.0 %all-reduce.5.cloned.1.call-start = ((), (), s32[]{:S(2)}) async-start(), calls=%async_computation | async-start | bytes 5079040 | tf_op jit(solution)/shard_map/psum | solution.py:334
  126.3 5.0 %collective-permute-start.9 = (bf16[496,2560]{1,0:T(8,128)(2,1)}, bf16[496,2560]{1,0:T(8,128)(2,1)S(1)}, u32[]{:S(2)}, u32[]{:S(2)}) collective-permute-start(bf16[496,2560]{1,0:T(8,128)(2,1)} %dynamic-slice_bitcast_fusion), channel_id=1, source_target_pairs={{0,1},{1,0},{2,3},{3,2},{4,5},{5,4},{6,7},{7,6},{8,9},{9,8},{10,11... | collective-permute-start | bytes 7618568 | tf_op jit(solution)/shard_map/ppermute | solution.py:213
  135.4 192.6 %copy-start.31 = (bf16[1280,960]{0,1:T(8,128)(2,1)S(1)}, bf16[1280,960]{0,1:T(8,128)(2,1)}, u32[]{:S(2)}) copy-start(bf16[1280,960]{0,1:T(8,128)(2,1)} %param.23) | copy-start | bytes 7372804
  331.0 4.4 copy-start.8
  331.0 4.4 copy-start.19
  (23 other events, 51.5 us)
Sparse Core Ops, SparseCore 0:
  88.6 239.3 all-reduce.6
  333.7 133.6 all-reduce.4

commit v3 on v2

--- a/solution.py
+++ b/solution.py
@@ -285,7 +285,6 @@
         returned(up_parts, shards),
         returned(down_parts, shards),
     )
-    ffn_sums = lax.psum(ffn_own, "replica")
     gain_two_part = jnp.sum(grad_hidden_two * normed_two, 0)
     grad_middle = upstream_grad.astype(jnp.float32) + norm_backward(
         grad_hidden_two * gain_two, normed_two, inverse_two
@@ -297,7 +296,6 @@
 
     output_part = contract(mixed, grad_middle_low, 1, 0)
     grad_mixed = contract(output_w, grad_middle_low, 1, 1).astype(jnp.bfloat16)
-    grad_mixed, _ = lax.optimization_barrier((grad_mixed, ffn_own))
     grad_query, grad_key, grad_value = attention_backward(
         segment, query, key, key_rows, value_rows, grad_mixed
     )
@@ -330,8 +328,8 @@
         )
         for step in range(shards)
     ]
-    packed, ffn_sums = lax.optimization_barrier((returned(packed, shards), ffn_sums))
-    packed = lax.psum(packed, "replica").astype(jnp.float32)
+    *ffn_sums, packed = lax.psum((*ffn_own, returned(packed, shards)), "replica")
+    packed = packed.astype(jnp.float32)
     gate_grad, up_grad, down_grad = [total.astype(jnp.float32) for total in ffn_sums]
     ends = [query_size, query_size + key_size, query_size + 2 * key_size]
     query_grad = packed[:rows, : ends[0]]

time: 489 us -> 468 us (0.957)
  waiting for transfers between devices: 321 us -> 288 us
  matrix products: 63.9 us -> 75.1 us
    psum x2 -> x1, waiting for transfers between devices: 314 us -> 286 us  [per_device(): lax.psum((*ffn_own, returned(packed, shards)), 'replica')]
    dot_general x6, matrix products: 13.4 us -> 24.6 us  [left_inner(): lax.dot_general(left, right, (((0,), (0,)), ((), ())), preferred_element_...]
    unnamed x74 -> x88, local copies, waits for them, and re-layouts: 14 us -> 12.6 us
  transfers between devices with their start and end apart: 12 -> 11, of which waited for: 5 -> 3; matrix products, arithmetic and copies ran while one was open for 18% -> 14% of each run, Pallas kernels for 6% -> 2%
where the time goes in v3:
time: 468 us; the launch traced here: 462 us
  waiting for transfers between devices  288 us (62%)
  matrix products  75.1 us (16%)
  Pallas kernels  28.8 us (6%)
  other arithmetic  28.5 us (6%)
  local copies, waits for them, and re-layouts  23.8 us (5%)
  between operations  14.9 us (3%)
    psum x1, waiting for transfers between devices, per_device(): lax.psum((*ffn_own, returned(packed, shards)), 'replica')  286 us
    dot_general x6, matrix products, left_inner(): lax.dot_general(left, right, (((0,), (0,)), ((), ())), preferred_element_...  24.6 us
    dot_general x6, matrix products, product(): return jnp.dot(left, right, preferred_element_type=jnp.float32)  19.8 us
    pallas_call x1, Pallas kernels, attention_backward(): pl.pallas_call(backward_kernel, grid=(KEY_VALUE_HEADS,), out_shape=(jax.S...  17.6 us
    dot_general x6, matrix products, right_inner(): lax.dot_general(left, right, (((1,), (1,)), ((), ())), preferred_element_...  16.7 us
    dot_general x6, matrix products, contract(): lax.dot_general(left, right, (((left_dim,), (right_dim,)), ((), ())), pre...  14 us
    unnamed x88, local copies, waits for them, and re-layouts  12.6 us
    pallas_call x1, Pallas kernels, attention_forward(): pl.pallas_call(forward_kernel, grid=(KEY_VALUE_HEADS,), out_shape=jax.Sha...  11.1 us
  transfers between devices with their start and end apart: 11, of which 3 were waited for; matrix products, arithmetic and copies ran while one was open for 14% of the time, Pallas kernels for 2%

profile of v3, /device:TPU:0, one launch (start us, length us, event | category | flops | bytes accessed | tf_op | source)
XLA Modules:
  0.0 462.0 jit_solution(15603323679078068961)
XLA Ops:
  18.4 2.9 broadcast_select_fusion.3
  26.4 11.1 %shard_map.203 = bf16[960,512]{1,0:T(8,128)(2,1)S(1)} custom-call(s32[512,1]{1,0:T(8,128)S(1)} %copy.48.seg_col, s32[1,512]{1,0:T(1,128)S(1)} %copy-done, bf16[960,512]{1,0:T(8,128)(2,1)S(1)} %bitcast.71, bf16[5,512,64]{2,1,0:T(8,128)(2,1)S(1)} %bitcast.73, bf16[320,512]{1,0:T(8,128)(2,1)S(1)} %slice.120.value), custom_call_target="tpu_custom_call" | custom-call | flops 4026531840 | bytes 3145728 | tf_op jit(solution)/shard_map/pallas_call | solution.py:153
  46.8 3.6 multiply_convert_fusion.2
  53.4 3.2 fusion.37
  56.6 3.2 fusion.34
  59.9 5.7 %multiply_convert_fusion.1 = (bf16[512,1280]{1,0:T(8,128)(2,1)S(1)}, bf16[512,1280]{1,0:T(8,128)(2,1)}, bf16[512,1280]{1,0:T(8,128)(2,1)S(1)}) fusion(f32[512,1280]{1,0:T(8,128)S(1)} %fusion.37, f32[512,1280]{1,0:T(8,128)S(1)} %fusion.34, bf16[512,960]{0,1:T(8,128)(2,1)S(1)} %multiply_convert_fusion.6, bf16[960,1280]{1,0:T(8,128)(2,1)} %collective-permute-done.3), kind=kOutput, calls=%fused_computation.22 | convolution fusion | flops 1268776960 | bytes 12615680 | tf_op jit(solution)/shard_map/dot_general | solution.py:21
  65.6 3.3 fusion.38
  68.9 3.6 multiply_reduce_fusion
  75.3 17.6 %shard_map.204 = (f32[960,512]{1,0:T(8,128)S(1)}, f32[320,512]{1,0:T(8,128)S(1)}, f32[320,512]{1,0:T(8,128)S(1)}) custom-call(s32[512,1]{1,0:T(8,128)S(1)} %copy.48.seg_col, s32[1,512]{1,0:T(1,128)S(1)} %copy-done, bf16[960,512]{1,0:T(8,128)(2,1)S(1)} %bitcast.72, bf16[320,512]{1,0:T(8,128)(2,1)S(1)} %bitcast.70, bf16[5,512,64]{2,1,0:T(8,128)(2,1)S(1)} %bitcast.74, ...), custom_call_target="tpu_custom_call" | custom-call | flops 10066329600 | bytes 8388608 | tf_op jit(solution)/shard_map/pallas_call | solution.py:170
  95.3 3.4 fusion.14
  98.7 3.7 convolution_convert_fusion.3
  102.4 2.9 convolution_convert_fusion.2
  105.3 2.9 convolution_convert_fusion.1
  109.0 4.3 convolution_convert_fusion
  115.6 3.8 fusion.1
  122.6 5.1 %add_convert_fusion.2 = bf16[960,1280]{1,0:T(8,128)(2,1)} fusion(bf16[960,1280]{1,0:T(8,128)(2,1)} %collective-permute-done.7, bf16[512,960]{0,1:T(8,128)(2,1)S(1)} %copy-done.7, bf16[512,1280]{1,0:T(8,128)(2,1)} %copy-done.39), kind=kOutput, calls=%fused_computation.8 | convolution fusion | flops 1261977600 | bytes 7208960 | tf_op jit(solution)/shard_map/dot_general | solution.py:25
  127.7 4.7 %add_convert_fusion.1 = bf16[960,1280]{1,0:T(8,128)(2,1)} fusion(bf16[960,1280]{1,0:T(8,128)(2,1)} %collective-permute-done.8, bf16[512,960]{0,1:T(8,128)(2,1)S(1)} %copy-done.7, bf16[512,1280]{1,0:T(8,128)(2,1)S(1)} %copy-done.38), kind=kOutput, calls=%fused_computation.7 | convolution fusion | flops 1261977600 | bytes 7208960 | tf_op jit(solution)/shard_map/dot_general | solution.py:25
  132.5 4.7 %add_convert_fusion = bf16[1280,960]{0,1:T(8,128)(2,1)} fusion(bf16[1280,960]{0,1:T(8,128)(2,1)} %collective-permute-done.9, bf16[512,960]{0,1:T(8,128)(2,1)S(1)} %copy-done.13, bf16[512,1280]{1,0:T(8,128)(2,1)S(1)} %copy-done.36), kind=kOutput, calls=%fused_computation.6 | convolution fusion | flops 1261977600 | bytes 7208960 | tf_op jit(solution)/shard_map/dot_general | solution.py:25
  137.1 3.8 fusion.2
  141.0 3.7 fusion.33
  147.4 4.1 add_convert_fusion.3
  151.5 285.9 %all-reduce.4.cloned.1.call-done = (bf16[496,2560]{1,0:T(8,128)(2,1)}, bf16[960,1280]{1,0:T(8,128)(2,1)}, bf16[960,1280]{1,0:T(8,128)(2,1)}, bf16[1280,960]{0,1:T(8,128)(2,1)}) async-done(((bf16[496,2560]{1,0:T(8,128)(2,1)}, bf16[960,1280]{1,0:T(8,128)(2,1)}, bf16[960,1280]{1,0:T(8,128)(2,1)}, bf16[1280,960]{0,1:T(8,128)(2,1)}), (bf16[496,2560]{1,0:T(8,128)(2,1)}, bf16[960,1280]{1,0:T(8,128)(2,1)}, ...) | async-done | bytes 9912336 | tf_op jit(solution)/shard_map/psum | solution.py:331
  438.8 4.1 fusion.29
  445.3 4.5 convert_element_type.171
  (164 shorter events, 51.3 us)
Async XLA Ops:
  7.2 430.2 %all-reduce.4.cloned.1.call-start = ((), (), s32[]{:S(2)}) async-start(), calls=%async_computation | async-start | bytes 19824640 | tf_op jit(solution)/shard_map/psum | solution.py:331
  8.4 5.1 %copy-start.32 = (bf16[480]{0:T(512)(128)(2,1)S(1)}, bf16[480]{0:T(512)(128)(2,1)}, u32[]{:S(2)}) copy-start(bf16[480]{0:T(512)(128)(2,1)} %param.20) | copy-start | bytes 2884
  8.5 5.1 %copy-start.33 = (bf16[480]{0:T(512)(128)(2,1)S(1)}, bf16[480]{0:T(512)(128)(2,1)}, u32[]{:S(2)}) copy-start(bf16[480]{0:T(512)(128)(2,1)} %param.15) | copy-start | bytes 2884
  8.5 6.2 %copy-start = (s32[1,512]{1,0:T(1,128)S(1)}, s32[1,512]{1,0:T(1,128)}, u32[]{:S(2)}) copy-start(s32[1,512]{1,0:T(1,128)} %seg_row.3) | copy-start | bytes 6148
  8.5 6.6 %copy-start.14 = (bf16[512,960]{0,1:T(8,128)(2,1)S(1)}, bf16[512,960]{0,1:T(8,128)(2,1)}, u32[]{:S(2)}) copy-start(bf16[512,960]{0,1:T(8,128)(2,1)} %param.12) | copy-start | bytes 2949124
  13.0 8.2 %collective-permute-start = (bf16[480,1600]{1,0:T(8,128)(2,1)S(1)}, bf16[480,1600]{1,0:T(8,128)(2,1)}, u32[]{:S(2)}, u32[]{:S(2)}) collective-permute-start(bf16[480,1600]{1,0:T(8,128)(2,1)S(1)} %concatenate.29), channel_id=1, source_target_pairs={{0,1},{1,0},{2,3},{3,2},{4,5},{5,4},{6,7},{7,6},{8,9},{9,8},{10,11... | collective-permute-start | bytes 4608008 | tf_op jit(solution)/shard_map/ppermute | solution.py:194
  13.6 2.9 collective-permute-start.1
  13.7 4.7 %collective-permute-start.2 = (bf16[480,960]{1,0:T(8,128)(2,1)}, bf16[480,960]{1,0:T(8,128)(2,1)}, u32[]{:S(2)}, u32[]{:S(2)}) collective-permute-start(bf16[480,960]{1,0:T(8,128)(2,1)} %param.19), channel_id=1, source_target_pairs={{0,1},{1,0},{2,3},{3,2},{4,5},{5,4},{6,7},{7,6},{8,9},{9,8},{10,11... | collective-permute-start | bytes 2764808 | tf_op jit(solution)/shard_map/ppermute | solution.py:194
  14.2 39.2 %collective-permute-start.5 = (bf16[1280,960]{0,1:T(8,128)(2,1)}, bf16[1280,960]{0,1:T(8,128)(2,1)}, u32[]{:S(2)}, u32[]{:S(2)}) collective-permute-start(bf16[1280,960]{0,1:T(8,128)(2,1)} %param.23), channel_id=1, source_target_pairs={{1,0},{0,1},{3,2},{2,3},{5,4},{4,5},{7,6},{6,7},{9,8},{8,9},{11,10... | collective-permute-start | bytes 7372808 | tf_op jit(solution)/shard_map/ppermute | solution.py:205
  14.2 42.4 %collective-permute-start.4 = (bf16[960,1280]{1,0:T(8,128)(2,1)}, bf16[960,1280]{1,0:T(8,128)(2,1)}, u32[]{:S(2)}, u32[]{:S(2)}) collective-permute-start(bf16[960,1280]{1,0:T(8,128)(2,1)} %param.22), channel_id=1, source_target_pairs={{1,0},{0,1},{3,2},{2,3},{5,4},{4,5},{7,6},{6,7},{9,8},{8,9},{11,10... | collective-permute-start | bytes 7372808 | tf_op jit(solution)/shard_map/ppermute | solution.py:205
  16.5 43.4 %collective-permute-start.3 = (bf16[960,1280]{1,0:T(8,128)(2,1)}, bf16[960,1280]{1,0:T(8,128)(2,1)}, u32[]{:S(2)}, u32[]{:S(2)}) collective-permute-start(bf16[960,1280]{1,0:T(8,128)(2,1)} %param.21), channel_id=1, source_target_pairs={{1,0},{0,1},{3,2},{2,3},{5,4},{4,5},{7,6},{6,7},{9,8},{8,9},{11,10... | collective-permute-start | bytes 7372808 | tf_op jit(solution)/shard_map/ppermute | solution.py:205
  26.3 11.2 %copy-start.15 = (bf16[512,960]{0,1:T(8,128)(2,1)S(1)}, bf16[512,960]{0,1:T(8,128)(2,1)}, u32[]{:S(2)}) copy-start(bf16[512,960]{0,1:T(8,128)(2,1)} %param.12) | copy-start | bytes 2949124
  26.3 11.2 %copy-start.28 = (bf16[480,960]{1,0:T(8,128)(2,1)S(1)}, bf16[480,960]{1,0:T(8,128)(2,1)}, u32[]{:S(2)}) copy-start(bf16[480,960]{1,0:T(8,128)(2,1)} %get-tuple-element.77) | copy-start | bytes 2764804
  26.3 11.2 %copy-start.30 = (bf16[480,960]{1,0:T(8,128)(2,1)S(1)}, bf16[480,960]{1,0:T(8,128)(2,1)}, u32[]{:S(2)}) copy-start(bf16[480,960]{1,0:T(8,128)(2,1)} %get-tuple-element.78) | copy-start | bytes 2764804
  42.7 62.6 %copy-start.6 = (bf16[512,960]{0,1:T(8,128)(2,1)}, bf16[512,960]{0,1:T(8,128)(2,1)S(1)}, u32[]{:S(2)}) copy-start(bf16[512,960]{0,1:T(8,128)(2,1)S(1)} %multiply_convert_fusion.6) | copy-start | bytes 2949124
  108.5 14.1 %collective-permute-start.7 = (bf16[960,1280]{1,0:T(8,128)(2,1)}, bf16[960,1280]{1,0:T(8,128)(2,1)}, u32[]{:S(2)}, u32[]{:S(2)}) collective-permute-start(bf16[960,1280]{1,0:T(8,128)(2,1)} %convolution_convert_fusion.2), channel_id=1, source_target_pairs={{0,1},{1,0},{2,3},{3,2},{4,5},{5,4},{6,7},{7,6},{8,9},{9,8},{10,11... | collective-permute-start | bytes 7372808 | tf_op jit(solution)/shard_map/ppermute | solution.py:213
  108.8 18.8 %collective-permute-start.8 = (bf16[960,1280]{1,0:T(8,128)(2,1)}, bf16[960,1280]{1,0:T(8,128)(2,1)}, u32[]{:S(2)}, u32[]{:S(2)}) collective-permute-start(bf16[960,1280]{1,0:T(8,128)(2,1)} %convolution_convert_fusion.1), channel_id=1, source_target_pairs={{0,1},{1,0},{2,3},{3,2},{4,5},{5,4},{6,7},{7,6},{8,9},{9,8},{10,11... | collective-permute-start | bytes 7372808 | tf_op jit(solution)/shard_map/ppermute | solution.py:213
  109.0 4.7 %copy-start.10 = (f32[512,960]{0,1:T(8,128)S(1)}, f32[512,960]{0,1:T(8,128)}, u32[]{:S(2)}) copy-start(f32[512,960]{0,1:T(8,128)} %copy-done.9) | copy-start | bytes 5898244
  113.3 19.1 %collective-permute-start.9 = (bf16[1280,960]{0,1:T(8,128)(2,1)}, bf16[1280,960]{0,1:T(8,128)(2,1)}, u32[]{:S(2)}, u32[]{:S(2)}) collective-permute-start(bf16[1280,960]{0,1:T(8,128)(2,1)} %convolution_convert_fusion), channel_id=1, source_target_pairs={{0,1},{1,0},{2,3},{3,2},{4,5},{5,4},{6,7},{7,6},{8,9},{9,8},{10,11... | collective-permute-start | bytes 7372808 | tf_op jit(solution)/shard_map/ppermute | solution.py:213
  122.5 14.7 %collective-permute-start.6 = (bf16[496,2560]{1,0:T(8,128)(2,1)}, bf16[496,2560]{1,0:T(8,128)(2,1)}, u32[]{:S(2)}, u32[]{:S(2)}) collective-permute-start(bf16[496,2560]{1,0:T(8,128)(2,1)} %dynamic-slice_bitcast_fusion), channel_id=1, source_target_pairs={{0,1},{1,0},{2,3},{3,2},{4,5},{5,4},{6,7},{7,6},{8,9},{9,8},{10,11... | collective-permute-start | bytes 7618568 | tf_op jit(solution)/shard_map/ppermute | solution.py:213
  122.6 5.1 %copy-start.38 = (bf16[512,1280]{1,0:T(8,128)(2,1)S(1)}, bf16[512,1280]{1,0:T(8,128)(2,1)}, u32[]{:S(2)}) copy-start(bf16[512,1280]{1,0:T(8,128)(2,1)} %copy-done.37) | copy-start | bytes 3932164
  127.7 4.8 %copy-start.13 = (bf16[512,960]{0,1:T(8,128)(2,1)S(1)}, bf16[512,960]{0,1:T(8,128)(2,1)}, u32[]{:S(2)}) copy-start(bf16[512,960]{0,1:T(8,128)(2,1)} %param.14) | copy-start | bytes 2949124
  127.7 4.8 %copy-start.36 = (bf16[512,1280]{1,0:T(8,128)(2,1)S(1)}, bf16[512,1280]{1,0:T(8,128)(2,1)}, u32[]{:S(2)}) copy-start(bf16[512,1280]{1,0:T(8,128)(2,1)} %get-tuple-element.61) | copy-start | bytes 3932164
  127.7 9.4 %slice-start = ((s8[5079040]{0:T(1024)(128)(4,1)}), s8[4194304]{0:T(1024)(128)(4,1)S(1)}, s32[]{:S(2)}) async-start(s8[5079040]{0:T(1024)(128)(4,1)} %bitcast.80), calls=%async_computation.1 | async-start | bytes 8388608
  (29 other events, 73.9 us)
Sparse Core Ops, SparseCore 0:
  141.1 296.2 all-reduce.3
